TPU v7x, 32 devices: a whole 2x2x4 slice. The times are simulated.
32 devices in a mesh: peer: 2 (over x), depth: 4 (over z), row: 4 (over y, core).
Axes of the slice: x: 2, y: 2, z: 4, core: 2. Of those that a mesh axis runs over, the one named last changes fastest.
Arguments:
- features: bfloat16 [12, 32, 2048], P('depth', 'row'), may hold values from -6 to 6
- labels: int32 [12, 32, 64], P('depth', 'row'), may hold values from 0 to 103
- conv_weights: bfloat16 [2, 4, 864, 32], P('peer'), may hold values from -0.21875 to 0.21875
- head_weights: bfloat16 [2, 32, 104], P('peer'), may hold values from -4 to 4
- matching: int32 [12, 2], P('depth'), may hold values from 0 to 1, each once within a row
Outputs:
- conv_grads: float32 [2, 4, 864, 32], P('peer')
- head_grads: float32 [2, 32, 104], P('peer')
- input_grads: bfloat16 [2, 12, 32, 2048], P('peer', 'depth', 'row')
Inputs may be any that keep to these rules, and one draw needn't show every extreme that they name: `matching`: in every depth plane every peer is distilled by exactly one peer.
All inputs are finite; a program needn't handle non-finite values.
Results may differ from a plain program's by a relative error of at most 0.019.
Values may be sent and summed in bfloat16 or wider, within the bound.
No kernel may reach another device: no remote copies, remote signals or barrier semaphores. Data moves between devices by JAX's collectives and lax.ppermute only.
A program may use at most 64 MiB of HBM per device.

v0:
```python
import functools

import jax
import jax.numpy as jnp
from jax import lax
from jax.experimental import pallas as pl
from jax.experimental.pallas import tpu as pltpu
from jax.sharding import PartitionSpec as P

LANES = 128
PAIR = 2 * LANES
F32 = jnp.float32
BF16 = jnp.bfloat16
GROUP = ("depth", "row")


def round_up(value, step):
    return -(-value // step) * step


class Plan:
    def __init__(self, mesh, features, labels, conv_weights, head_weights):
        self.n_depth = mesh.shape["depth"]
        self.n_row = mesh.shape["row"]
        self.n_peer = mesh.shape["peer"]
        self.n = self.n_depth * self.n_row
        self.slab_depth, self.slab_rows, merged = features.shape
        self.layers, self.taps, self.channels = conv_weights.shape[1:]
        self.classes = head_weights.shape[2]
        self.width = merged // self.channels
        self.depth = self.slab_depth * self.n_depth
        self.rows = self.slab_rows * self.n_row
        self.m = self.depth * self.rows
        self.slab = self.slab_depth * self.slab_rows
        self.own = self.width // self.n
        self.group = LANES // self.channels
        self.halo = 2 * self.layers
        self.blocks = round_up(2 * self.halo + self.own, self.group) // self.group
        self.window = self.blocks * self.group
        self.top = self.window - 2 * self.layers
        self.top_blocks = round_up(self.top, self.group) // self.group
        self.lane_blocks = round_up(self.taps, LANES) // LANES
        spare = self.lane_blocks * LANES - self.taps
        self.spare = spare if spare * self.layers >= self.classes else 0
        self.grad_rows = (self.layers * self.lane_blocks + (0 if self.spare else 1)) * self.channels
        self.chunk = round_up(-(-self.grad_rows // self.n), 8)
        self.back_rows = round_up(self.chunk + self.slab, 8)


def crop_mask(block, level, base, plan):
    place = base + block * plan.group + level + lax.broadcasted_iota(jnp.int32, (1, LANES), 1) // plan.channels
    return (place >= 0) & (place < plan.width)


def first_half():
    return lax.broadcasted_iota(jnp.int32, (1, LANES), 1) < LANES // 2


def position(plan):
    return lax.axis_index("depth") * plan.n_row + lax.axis_index("row")


def clear_edges(xs, plan):
    rows = plan.rows
    zero = jnp.zeros((rows, LANES), BF16)
    for slot in range(xs.shape[0]):
        xs[slot, 0:rows, :] = zero
        xs[slot, rows + plan.m : 2 * rows + plan.m, :] = zero


def fill_odd(xs, slots, plan):
    at = slice(plan.rows, plan.rows + plan.m)
    for t in slots:
        xs[t, at, :] = jnp.where(first_half(), xs[t + 1, at, :], xs[t - 1, at, :])


def convolve(xs, slots, matrix, plan):
    m, rows = plan.m, plan.rows
    row = lax.rem(lax.broadcasted_iota(jnp.int32, (m, 1), 0), rows)
    parts = []
    for half, slot in enumerate(slots):
        if slot is None:
            parts.append(None)
            continue
        lhs = jnp.concatenate([xs[slot, i * rows : i * rows + m, :] for i in range(3)], axis=1)
        parts.append(jnp.dot(lhs, matrix(half), preferred_element_type=F32))
    left, right = (parts[0] if parts[0] is not None else parts[1]), (parts[1] if parts[1] is not None else parts[0])
    mask = first_half()
    center = jnp.where(mask, left[:, :LANES], right[:, :LANES])
    before = pltpu.roll(jnp.where(mask, right[:, :LANES], left[:, :LANES]), LANES // 2, 1)
    after = jnp.where(mask, left[:, LANES:], right[:, LANES:])
    before = jnp.where(row == 0, 0.0, pltpu.roll(before, 1, 0))
    after = jnp.where(row == rows - 1, 0.0, pltpu.roll(after, m - 1, 0))
    return before + center + after


SLOTS = ({1: 0, 0: 2, 2: 4}, {0: 0, 1: 2, 2: 6})


def lane_masks(plan):
    place = lax.broadcasted_iota(jnp.int32, (plan.channels, PAIR), 1) // plan.channels
    return [(place == q).astype(BF16) for q in range(PAIR // plan.channels)]


def band_rows(term, forward, i, p, half, masks):
    turned = (half == 1) if forward else (half == 0)
    f = (p - 2) % 4 if turned else p
    total = None
    for o in range(2):
        k = f - o if forward else o + 2 - f
        if not 0 <= k <= 2:
            continue
        for j in range(3):
            ij = 3 * i + j if forward else 3 * (2 - i) + 2 - j
            piece = term(3 * ij + k) * masks[SLOTS[half][j] + o]
            total = piece if total is None else total + piece
    return total


def band_kernel(plan, peers, backward, turned_ref, *refs):
    ch, group = plan.channels, plan.group
    outs, (wide, tall) = refs[:-2], refs[-2:]
    eye_r = lax.broadcasted_iota(jnp.int32, (ch, PAIR), 0)
    eye_l = lax.broadcasted_iota(jnp.int32, (ch, PAIR), 1)
    spread = (eye_r == lax.rem(eye_l, ch)).astype(BF16)
    zero = jnp.zeros_like(spread)
    spreads = jnp.concatenate(
        [jnp.concatenate([spread if u == v else zero for u in range(group)], axis=1) for v in range(group)], axis=0
    )
    masks = lane_masks(plan)
    for peer in range(peers):
        for layer in range(plan.layers):
            weights = turned_ref[peer, layer]
            wide[layer] = lax.dot_general(
                weights, spread, (((0,), (0,)), ((), ())), preferred_element_type=F32
            ).astype(BF16)
            for q in range(plan.lane_blocks if backward else 0):
                count = min(LANES, plan.taps - q * LANES)
                part = jnp.dot(
                    weights[:, q * LANES : q * LANES + count], spreads[0:count], preferred_element_type=F32
                ).astype(BF16)
                for u in range(count // ch):
                    tall[layer, q * group + u] = part[:, u * PAIR : (u + 1) * PAIR]

        def one(layer, carry, peer=peer):
            for half in range(2):
                for i in range(3):
                    for p in range(group):
                        at = slice((i * group + p) * ch, (i * group + p + 1) * ch)
                        outs[0][peer, layer, half, at, :] = band_rows(
                            lambda n: wide[layer, n * ch : (n + 1) * ch, :], True, i, p, half, masks
                        )
                        if backward:
                            outs[1][peer, layer, half, at, :] = band_rows(
                                lambda n: tall[layer, n], False, i, p, half, masks
                            )
            return carry

        lax.fori_loop(0, plan.layers, one, 0)


def head_matrix(head, plan):
    ch, group = plan.channels, plan.group
    lanes = lax.broadcasted_iota(jnp.int32, (ch, group * LANES), 1) // LANES
    wide = jnp.concatenate([head] * group, axis=1)
    zero = jnp.zeros_like(wide)
    return jnp.concatenate([jnp.where(lanes == v, wide, zero) for v in range(group)], axis=0)


def pack_kernel(plan, match_hbm, feat_hbm, label_hbm, out_ref, match_ref, feat_ref, label_ref, sems):
    ch, own = plan.channels, plan.own
    copies = [
        pltpu.make_async_copy(source, target, sems.at[n])
        for n, (source, target) in enumerate(((feat_hbm, feat_ref), (label_hbm, label_ref), (match_hbm, match_ref)))
    ]
    for copy in copies:
        copy.start()
    for copy in copies:
        copy.wait()
    feats = feat_ref[...].astype(F32).reshape(plan.slab, plan.width * ch)
    labels = label_ref[...].astype(F32)
    peer = lax.axis_index("peer")
    lane = lax.broadcasted_iota(jnp.int32, (plan.slab_rows, LANES), 1)
    seen = 3 * plan.group
    matches = jnp.zeros((plan.slab_rows, LANES), F32)
    for k in range(plan.slab_depth):
        matches = jnp.where(lane == LANES - plan.slab_depth + k, match_ref[peer, k].astype(F32), matches)

    def cut(array, low, high, limit):
        pieces = []
        if low < 0:
            pieces.append(jnp.zeros((array.shape[0], min(-low, high - low)), F32))
        if max(low, 0) < min(high, limit):
            pieces.append(array[:, max(low, 0) : min(high, limit)])
        if high > limit:
            pieces.append(jnp.zeros((array.shape[0], min(high - limit, high - low)), F32))
        return jnp.concatenate(pieces, axis=1) if len(pieces) > 1 else pieces[0]

    for p in range(plan.n):
        first = p * own - plan.halo
        parts = []
        for q in range(plan.blocks):
            low = (first + q * plan.group) * ch
            parts.append(cut(feats, low, low + LANES, plan.width * ch))
        low = p * own + plan.layers - plan.halo
        pieces = []
        for k in range(plan.slab_depth):
            pieces.append(cut(labels[k], low, low + seen, plan.width))
        pieces.append(jnp.zeros((plan.slab_rows, LANES - plan.slab_depth * seen), F32))
        parts.append(jnp.concatenate(pieces, axis=1) + matches)
        out_ref[p] = jnp.concatenate(parts, axis=0).astype(BF16)


def unpack_slabs(plan, recv_ref, source, label_ref):
    rows = plan.rows
    lane = lax.broadcasted_iota(jnp.int32, (1, LANES), 1)
    seen = 3 * plan.group
    keep = LANES - plan.slab_depth
    for d in range(plan.n_depth):
        parts = [recv_ref[d * plan.n_row + r].astype(F32) for r in range(plan.n_row)]
        for k in range(plan.slab_depth):
            at = (d * plan.slab_depth + k) * rows
            for q in range(plan.blocks + 1):
                low = q * plan.slab + k * plan.slab_rows if q < plan.blocks else plan.blocks * plan.slab
                piece = jnp.concatenate([x[low : low + plan.slab_rows] for x in parts], axis=0)
                if q < plan.blocks:
                    source[2 * q, rows + at : rows + at + rows, :] = piece.astype(BF16)
                    continue
                if k > 0:
                    moved = pltpu.roll(piece, LANES - k * seen, 1)
                    piece = jnp.where(lane < seen, moved, pltpu.roll(piece, LANES - k, 1))
                label_ref[at : at + rows, :] = jnp.where((lane < seen) | (lane == keep), piece, 0.0)


def forward(plan, buffers, first, matrix, base, keep):
    m, rows, group = plan.m, plan.rows, plan.group
    at = slice(rows, rows + m)
    count = plan.window
    source = buffers[first]
    for layer in range(plan.layers):
        target = buffers[1 + layer % 2]
        fill_odd(source, range(1, (count - 4) // 2 + 1, 2), plan)
        keep(layer, source)
        count -= 2
        for b in range(round_up(count, group) // group):
            slots = (2 * b, 2 * b + 1 if b * group + 2 < count else None)
            total = convolve(source, slots, lambda half: matrix(layer, half), plan)
            keep(layer, None, b, total)
            value = total / (1.0 + jnp.exp(-total))
            target[2 * b, at, :] = jnp.where(crop_mask(b, layer + 1, base, plan), value, 0.0).astype(BF16)
        source = target
    return source


def class_ones(plan):
    rows = lax.broadcasted_iota(jnp.int32, (2 * LANES, 2 * LANES), 0)
    lanes = lax.broadcasted_iota(jnp.int32, (2 * LANES, 2 * LANES), 1)
    return (rows // LANES == lanes // LANES).astype(BF16)


def probabilities(act, matrix, ones, plan):
    logits = jnp.dot(act, matrix, preferred_element_type=F32)
    lane = lax.rem(lax.broadcasted_iota(jnp.int32, (1, 2 * LANES), 1), LANES)
    probs = []
    for v in range(0, plan.group, 2):
        exponent = jnp.where(lane < plan.classes, jnp.exp(logits[:, v * LANES : (v + 2) * LANES]), 0.0)
        high = exponent.astype(BF16)
        rest = (exponent - high.astype(F32)).astype(BF16)
        total = jnp.dot(high, ones, preferred_element_type=F32) + jnp.dot(rest, ones, preferred_element_type=F32)
        probs.append(exponent / total)
    return probs


def main_kernel(plan, recv_ref, band_hbm, back_hbm, other_hbm, head_ref, heads_ref, out_ref, *scratch):
    slabs, one_xs, two_xs, acts, pres, label_ref, part, dlog, grads, band, back_band, other_band, sems = scratch
    ch, m, rows, group, own, layers = plan.channels, plan.m, plan.rows, plan.group, plan.own, plan.layers
    base = position(plan) * own - plan.halo
    peer = lax.axis_index("peer")
    copies = [pltpu.make_async_copy(band_hbm.at[0, n], band.at[n], sems.at[n]) for n in range(layers)]
    copies.append(pltpu.make_async_copy(back_hbm.at[0], back_band, sems.at[layers]))
    first = pltpu.make_async_copy(other_hbm.at[0], other_band, sems.at[layers + 1])
    for copy in copies:
        copy.start()
    first.start()
    buffers = (slabs, one_xs, two_xs)
    for xs in buffers:
        clear_edges(xs, plan)
    unpack_slabs(plan, recv_ref, slabs, label_ref)
    at = slice(rows, rows + m)
    lane = lax.broadcasted_iota(jnp.int32, (1, LANES), 1)
    half_mask = first_half()

    def keep(layer, source, b=None, total=None):
        if source is not None:
            copies[layer].wait()
            if layer == 0:
                acts[0, :, 0:LANES] = jnp.where(half_mask, source[6, at, :], source[2, at, :])
            else:
                acts[layer, :, 0:LANES] = source[2, at, :]
            acts[layer, :, LANES:PAIR] = source[4, at, :]
        elif b < plan.top_blocks:
            pres[layer, b] = total.astype(BF16)

    last = forward(plan, buffers, 0, lambda layer, half: band[layer, half], base, keep)
    own_matrix = head_matrix(head_ref[...], plan)
    ones = class_ones(plan)
    pair_lane = lax.rem(lax.broadcasted_iota(jnp.int32, (1, PAIR), 1), LANES).astype(F32)
    spread_r = lax.broadcasted_iota(jnp.int32, (LANES, PAIR), 0)
    spread_l = lax.broadcasted_iota(jnp.int32, (LANES, PAIR), 1) // LANES
    labels = label_ref[...]
    codes = labels.astype(BF16)
    match = labels[:, LANES - plan.slab_depth : LANES - plan.slab_depth + 1]
    weight = jnp.where(match == peer.astype(F32), 0.5, 0.0)
    for g in range(3):
        for u, value in enumerate(probabilities(last[2 * g, at, :], own_matrix, ones, plan)):
            place = g * group + 2 * u
            spread = (spread_r == spread_l + place).astype(BF16)
            label = jnp.dot(codes, spread, preferred_element_type=F32)
            onehot = jnp.where(label == pair_lane, 0.5, 0.0)
            part[:, place * LANES : place * LANES + PAIR] = (
                value - onehot - weight * value.astype(BF16).astype(F32)
            )
    hidden = last[2, at, :]

    def other(q, carry):
        if plan.n_peer > 2:

            @pl.when(q > 0)
            def fetch():
                copy = pltpu.make_async_copy(other_hbm.at[q], other_band, sems.at[layers + 2])
                copy.start()
                copy.wait()

        owner = lax.rem(peer - q - 1 + plan.n_peer, plan.n_peer)
        last = forward(plan, buffers, 0, lambda layer, half: other_band[layer, half], base, lambda *unused: None)
        matrix = head_matrix(heads_ref[q], plan)
        weight = jnp.where(match == owner.astype(F32), 0.5, 0.0)
        for g in range(3):
            for u, value in enumerate(probabilities(last[2 * g, at, :], matrix, ones, plan)):
                cols = slice((g * group + 2 * u) * LANES, (g * group + 2 * u + 2) * LANES)
                part[:, cols] = part[:, cols] - weight * value.astype(BF16).astype(F32)
        return carry

    first.wait()
    if plan.n_peer == 2:
        other(0, 0)
    else:
        lax.fori_loop(0, plan.n_peer - 1, other, 0)

    wide = group * LANES
    dlog[...] = part[...].astype(BF16)
    level = one_xs
    for g in range(3):
        back = lax.dot_general(
            dlog[:, g * wide : (g + 1) * wide], own_matrix, (((1,), (1,)), ((), ())), preferred_element_type=F32
        )
        value = jnp.where(crop_mask(g, layers, base, plan), back * slope(pres[layers - 1, g]), 0.0)
        level[2 * g, at, :] = value.astype(BF16)
    product = lax.dot_general(
        hidden, dlog[:, wide : 2 * wide], (((0,), (0,)), ((), ())), preferred_element_type=F32
    )
    head_grad = jnp.zeros((ch, LANES), F32)
    for v in range(own):
        head_grad = head_grad + product[v * ch : (v + 1) * ch, v * LANES : (v + 1) * LANES]
    if not plan.spare:
        low = layers * plan.lane_blocks * ch
        grads[low : low + ch, :] = head_grad
    if plan.n * plan.chunk > plan.grad_rows:
        grads[plan.grad_rows :, :] = jnp.zeros((plan.n * plan.chunk - plan.grad_rows, LANES), F32)

    row = lax.rem(lax.broadcasted_iota(jnp.int32, (m, 1), 0), rows)
    wide_lane = lax.broadcasted_iota(jnp.int32, (1, PAIR), 1)
    copies[layers].wait()
    for layer in reversed(range(layers)):
        u = plan.halo - layer - 1
        place = lax.rem(lane // ch - u % group + group, group)
        center = level[2 * (u // group), at, :].astype(F32)
        if u % group:
            center = jnp.where(lane // ch >= u % group, center, level[2 * (u // group) + 2, at, :].astype(F32))
        if own < group:
            center = jnp.where(place < own, center, 0.0)
        shifted = [
            jnp.where(row == rows - 1, 0.0, pltpu.roll(center, m - 1, 0)),
            center,
            jnp.where(row == 0, 0.0, pltpu.roll(center, 1, 0)),
        ]
        turned = jnp.concatenate([x.T.astype(BF16) for x in shifted], axis=0)
        slabs[0, at, :] = acts[layer, :, 0:LANES]
        slabs[1, at, :] = acts[layer, :, LANES:PAIR]
        blocks = [jnp.zeros((ch, PAIR), F32) for unused in range(round_up(plan.lane_blocks, 2) // 2)]
        for i in range(3):
            rhs = jnp.concatenate([slabs[n, i * rows : i * rows + m, :] for n in range(2)], axis=1)
            product = jnp.dot(turned, rhs, preferred_element_type=F32)
            for j in range(3):
                target = (3 * i + j) * 3 * ch
                total = None
                for b in range(own):
                    shift = (target - ((plan.halo + b - 1 - layer - group) % (2 * group)) * ch) % PAIR
                    low = j * LANES + ((u + b) % group) * ch
                    piece = product[low : low + ch]
                    piece = pltpu.roll(piece, shift, 1) if shift else piece
                    total = piece if total is None else total + piece
                for q in range(target // PAIR, (target + 3 * ch - 1) // PAIR + 1):
                    spot = wide_lane + q * PAIR
                    blocks[q] = jnp.where((spot >= target) & (spot < target + 3 * ch), total, blocks[q])
        for q in range(plan.lane_blocks):
            low = (layer * plan.lane_blocks + q) * ch
            block = blocks[q // 2][:, (q % 2) * LANES : (q % 2 + 1) * LANES]
            if plan.spare and q == plan.lane_blocks - 1:
                moved = pltpu.roll(head_grad, (LANES - plan.spare - layer * plan.spare) % LANES, 1)
                block = jnp.where(lane < LANES - plan.spare, block, moved)
            grads[low : low + ch, :] = block
        start = 2 * (layers - layer)
        target = two_xs if level is one_xs else one_xs
        fill_odd(level, [t for t in range(start // 2 - 1, plan.top // 2 - 1) if t % 2], plan)
        for b in range(start // group, plan.top_blocks):
            slots = (2 * b - 1 if b * group >= start else None, 2 * b)
            total = convolve(level, slots, lambda half: back_band[layer, half], plan)
            if layer > 0:
                total = total * slope(pres[layer - 1, b])
                target[2 * b, at, :] = jnp.where(crop_mask(b, layer, base, plan), total, 0.0).astype(BF16)
            else:
                result = total
        level = target

    for d in range(plan.n_depth):
        for r in range(plan.n_row):
            p = d * plan.n_row + r
            parts = [grads[p * plan.chunk : (p + 1) * plan.chunk, :]]
            for k in range(plan.slab_depth):
                low = (d * plan.slab_depth + k) * rows + r * plan.slab_rows
                parts.append(result[low : low + plan.slab_rows])
            spare = plan.back_rows - plan.chunk - plan.slab
            if spare:
                parts.append(jnp.zeros((spare, LANES), F32))
            out_ref[p] = jnp.concatenate(parts, axis=0).astype(BF16)


def slope(pre):
    value = pre.astype(F32)
    sigma = 1.0 / (1.0 + jnp.exp(-value))
    return sigma * (1.0 + value * (1.0 - sigma))


def sum_kernel(plan, recv_ref, out_ref, back_ref):
    total = None
    backs = []
    for p in range(plan.n):
        value = recv_ref[p].astype(F32)
        part = value[0 : plan.chunk]
        total = part if total is None else total + part
        backs.append(value[plan.chunk : plan.chunk + plan.slab])
    total = total.astype(BF16)
    for p in range(plan.n):
        out_ref[p] = total
    lanes = plan.own * plan.channels
    step = LANES // lanes
    for q in range(plan.n // step):
        pieces = [backs[q * step + u][:, 0:lanes] for u in range(step)]
        piece = pieces[0] if step == 1 else jnp.concatenate(pieces, axis=1)
        for k in range(plan.slab_depth):
            rows = piece[k * plan.slab_rows : (k + 1) * plan.slab_rows]
            back_ref[k, :, q * LANES : (q + 1) * LANES] = rows.astype(BF16)


def unpack_kernel(plan, recv_ref, conv_ref, head_ref):
    ch = plan.channels
    flat = jnp.concatenate([recv_ref[p].astype(F32) for p in range(plan.n)], axis=0)
    lane = lax.broadcasted_iota(jnp.int32, (1, LANES), 1)
    head = flat[plan.layers * plan.lane_blocks * ch :][0:ch] if not plan.spare else jnp.zeros((ch, LANES), F32)
    for layer in range(plan.layers):
        for q in range(plan.lane_blocks):
            at = (layer * plan.lane_blocks + q) * ch
            count = min(LANES, plan.taps - q * LANES)
            block = flat[at : at + ch]
            conv_ref[0, layer, :, q * LANES : q * LANES + count] = block[:, 0:count]
            if plan.spare and q == plan.lane_blocks - 1:
                moved = pltpu.roll(block, (plan.spare + layer * plan.spare) % LANES, 1)
                head = jnp.where((lane >= layer * plan.spare) & (lane < (layer + 1) * plan.spare), moved, head)
    head_ref[0] = head[:, 0 : plan.classes]


def hbm(array):
    return pltpu.with_memory_space_constraint(array, pltpu.HBM)


def call(kernel, plan, out_shape, scratch=(), specs=(True,), cost=None, limit=16):
    vmem = pl.BlockSpec(memory_space=pltpu.VMEM)
    anywhere = pl.BlockSpec(memory_space=pl.ANY)
    many = isinstance(out_shape, (list, tuple))
    return pl.pallas_call(
        functools.partial(kernel, plan),
        out_shape=out_shape,
        in_specs=[vmem if x else anywhere for x in specs],
        out_specs=[vmem] * len(out_shape) if many else vmem,
        scratch_shapes=list(scratch),
        compiler_params=pltpu.CompilerParams(vmem_limit_bytes=limit * 1024 * 1024),
        cost_estimate=cost,
    )


def make_bands(plan, turned, backward):
    peers = turned.shape[0]
    shape = jax.ShapeDtypeStruct((peers, plan.layers, 2, 3 * LANES, PAIR), BF16)
    made = call(
        lambda plan, *refs: band_kernel(plan, peers, backward, *refs),
        plan,
        [shape] * (2 if backward else 1),
        [
            pltpu.VMEM((plan.layers, plan.taps, PAIR), BF16),
            pltpu.VMEM((plan.layers, plan.taps // plan.channels, plan.channels, PAIR), BF16),
        ],
        cost=pl.CostEstimate(flops=10**9, bytes_accessed=4 * 10**6, transcendentals=0),
    )(turned)
    return [hbm(x) for x in made]


def from_others(array, peers):
    moved = [lax.ppermute(array, "peer", [(i, (i + q) % peers) for i in range(peers)]) for q in range(1, peers)]
    return moved[0] if len(moved) == 1 else jnp.concatenate(moved, axis=0)


def body(mesh, features, labels, conv_weights, head_weights, matching):
    plan = Plan(mesh, features, labels, conv_weights, head_weights)
    shape = jax.ShapeDtypeStruct
    m, ch, n, layers = plan.m, plan.channels, plan.n, plan.layers
    head = jnp.pad(head_weights, ((0, 0), (0, 0), (0, LANES - plan.classes)))
    chunk_rows = plan.blocks * plan.slab + plan.slab_rows
    packed = call(
        pack_kernel,
        plan,
        shape((n, chunk_rows, LANES), BF16),
        [
            pltpu.SMEM(matching.shape[::-1], jnp.int32),
            pltpu.VMEM(features.shape, BF16),
            pltpu.VMEM(labels.shape, jnp.int32),
            pltpu.SemaphoreType.DMA((3,)),
        ],
        specs=(False,) * 3,
    )(hbm(matching.T), hbm(features), hbm(labels))
    slabs = lax.all_to_all(packed, GROUP, 0, 0, tiled=True)
    turned = jnp.swapaxes(conv_weights, 2, 3)
    others = from_others(turned, plan.n_peer)
    heads = from_others(head, plan.n_peer)
    band, back_band = make_bands(plan, turned, True)
    (other_band,) = make_bands(plan, others, False)
    padded = m + 2 * plan.rows
    wide = 3 * plan.group * LANES
    windows = 2 * plan.blocks
    banded = pltpu.VMEM((layers, 2, 3 * LANES, PAIR), BF16)
    parts = call(
        main_kernel,
        plan,
        shape((n, plan.back_rows, LANES), BF16),
        [
            pltpu.VMEM((windows, padded, LANES), BF16),
            pltpu.VMEM((windows, padded, LANES), BF16),
            pltpu.VMEM((windows, padded, LANES), BF16),
            pltpu.VMEM((layers, m, PAIR), BF16),
            pltpu.VMEM((layers, plan.top_blocks, m, LANES), BF16),
            pltpu.VMEM((m, LANES), F32),
            pltpu.VMEM((m, wide), F32),
            pltpu.VMEM((m, wide), BF16),
            pltpu.VMEM((n * plan.chunk, LANES), F32),
            banded,
            banded,
            banded,
            pltpu.SemaphoreType.DMA((layers + 3,)),
        ],
        specs=(True, False, False, False, True, True),
        limit=48,
    )(slabs, band, back_band, other_band, head[0], heads)
    parts = lax.all_to_all(parts, GROUP, 0, 0, tiled=True)
    sums, input_grads = call(
        sum_kernel,
        plan,
        [shape((n, plan.chunk, LANES), BF16), shape(features.shape, BF16)],
    )(parts)
    sums = lax.all_to_all(sums, GROUP, 0, 0, tiled=True)
    conv_grads, head_grads = call(
        unpack_kernel,
        plan,
        [shape((1, layers, ch, plan.taps), F32), shape((1, ch, plan.classes), F32)],
    )(sums)
    return jnp.swapaxes(conv_grads, 2, 3), head_grads, input_grads[None]


def solution(mesh):
    placed = (
        P("depth", "row", None),
        P("depth", "row", None),
        P("peer", None, None, None),
        P("peer", None, None),
        P("depth", None),
    )
    return jax.shard_map(
        functools.partial(body, mesh),
        mesh=mesh,
        in_specs=placed,
        out_specs=(
            P("peer", None, None, None),
            P("peer", None, None),
            P("peer", "depth", "row", None),
        ),
        check_vma=False,
    )
```

profile of v0, /device:TPU:0, one launch (start us, length us, event | category | flops | bytes accessed | tf_op | source)
XLA Modules:
  0.0 71.4 jit_solution(16064794827063910140)
XLA Ops:
  0.6 0.0 copy-start.3
  0.6 0.0 copy-start.4
  0.7 1.9 %shard_map.76 = bf16[16,128,128]{2,1,0:T(8,128)(2,1)} custom-call(s32[2,3]{1,0:T(2,128)} %bitcast.8, bf16[3,8,2048]{2,1,0:T(8,128)(2,1)} %feat_hbm.1, s32[3,8,64]{2,1,0:T(8,128)} %label_hbm.1), custom_call_target="tpu_custom_call" | custom-call | tf_op jit(solution)/shard_map/pallas_call | solution.py:529
  2.6 7.4 %all-to-all-start = ((bf16[16,128,128]{2,1,0:T(8,128)(2,1)}), bf16[16,128,128]{2,1,0:T(8,128)(2,1)S(1)}, u32[]{:S(2)}, u32[]{:S(2)}) async-start(bf16[16,128,128]{2,1,0:T(8,128)(2,1)} %shard_map.76), calls=%async_computation | async-start | bytes 1048576 | tf_op jit(solution)/shard_map/all_to_all | solution.py:541
  10.0 0.0 copy-done.3
  10.0 1.6 %collective-permute-start = (bf16[1,4,32,864]{3,2,1,0:T(8,128)(2,1)S(1)}, bf16[1,4,32,864]{3,2,1,0:T(8,128)(2,1)S(1)}, u32[]{:S(2)}, u32[]{:S(2)}) collective-permute-start(bf16[1,4,32,864]{3,2,1,0:T(8,128)(2,1)S(1)} %bitcast.6), channel_id=1, source_target_pairs={{0,16},{16,0},{1,17},{17,1},{2,18},{18,2},{3,19},{19,3},{4,20},{20... | collective-permute-start | bytes 663560 | tf_op jit(solution)/shard_map/ppermute | solution.py:519
  11.5 0.0 copy-done.4
  11.6 0.6 collective-permute-start.1
  12.2 2.1 %shard_map.77 = (bf16[1,4,2,384,256]{4,3,2,1,0:T(8,128)(2,1)S(1)}, bf16[1,4,2,384,256]{4,3,2,1,0:T(8,128)(2,1)S(1)}) custom-call(bf16[1,4,32,864]{3,2,1,0:T(8,128)(2,1)S(1)} %bitcast.7), custom_call_target="tpu_custom_call" | custom-call | flops 1000000000 | bytes 4000000 | tf_op jit(solution)/shard_map/pallas_call | solution.py:505
  14.3 0.0 copy-start
  14.3 1.2 %copy-done = bf16[1,4,2,384,256]{4,3,2,1,0:T(8,128)(2,1)} copy-done((bf16[1,4,2,384,256]{4,3,2,1,0:T(8,128)(2,1)}, bf16[1,4,2,384,256]{4,3,2,1,0:T(8,128)(2,1)S(1)}, u32[]{:S(2)}) %copy-start) | copy-done | bytes 1572888
  15.4 0.0 copy-start.1
  15.4 2.6 %collective-permute-done.refs_0_ = bf16[1,4,32,864]{3,2,1,0:T(8,128)(2,1)S(1)} collective-permute-done((bf16[1,4,32,864]{3,2,1,0:T(8,128)(2,1)S(1)}, bf16[1,4,32,864]{3,2,1,0:T(8,128)(2,1)S(1)}, u32[]{:S(2)}, u32[]{:S(2)}) %collective-permute-start) | collective-permute-done | bytes 221216 | tf_op jit(solution)/shard_map/ppermute | solution.py:519
  18.1 1.3 %shard_map.78.other_hbm = bf16[1,4,2,384,256]{4,3,2,1,0:T(8,128)(2,1)S(1)} custom-call(bf16[1,4,32,864]{3,2,1,0:T(8,128)(2,1)S(1)} %collective-permute-done.refs_0_), custom_call_target="tpu_custom_call" | custom-call | flops 1000000000 | bytes 4000000 | tf_op jit(solution)/shard_map/pallas_call | solution.py:505
  19.4 0.0 copy-done.1
  19.4 0.0 copy-start.2
  19.4 1.1 %copy-done.2 = bf16[1,4,2,384,256]{4,3,2,1,0:T(8,128)(2,1)} copy-done((bf16[1,4,2,384,256]{4,3,2,1,0:T(8,128)(2,1)}, bf16[1,4,2,384,256]{4,3,2,1,0:T(8,128)(2,1)S(1)}, u32[]{:S(2)}) %copy-start.2) | copy-done | bytes 1572888
  20.5 0.0 collective-permute-done.1.heads_ref
  20.5 3.9 %all-to-all-done.recv_ref = bf16[16,128,128]{2,1,0:T(8,128)(2,1)S(1)} async-done(((bf16[16,128,128]{2,1,0:T(8,128)(2,1)}), bf16[16,128,128]{2,1,0:T(8,128)(2,1)S(1)}, u32[]{:S(2)}, u32[]{:S(2)}) %all-to-all-start) | async-done | bytes 524320 | tf_op jit(solution)/shard_map/all_to_all | solution.py:541
  24.4 17.9 %shard_map.79 = bf16[16,80,128]{2,1,0:T(8,128)(2,1)S(1)} custom-call(bf16[16,128,128]{2,1,0:T(8,128)(2,1)S(1)} %all-to-all-done.recv_ref, bf16[1,4,2,384,256]{4,3,2,1,0:T(8,128)(2,1)} %copy-done, bf16[1,4,2,384,256]{4,3,2,1,0:T(8,128)(2,1)} %copy-done.1, bf16[1,4,2,384,256]{4,3,2,1,0:T(8,128)(2,1)} %copy-done.2, ...), custom_call_target="tpu_custom_call" | custom-call | tf_op jit(solution)/shard_map/pallas_call | solution.py:551
  42.4 15.0 %all_to_all.15.recv_ref = bf16[16,80,128]{2,1,0:T(8,128)(2,1)S(1)} all-to-all(bf16[16,80,128]{2,1,0:T(8,128)(2,1)S(1)} %shard_map.79), channel_id=1, replica_groups=mesh['peer'=2,'depth'=4,'row'=4] {'depth','row'}, dimensions={0} | all-to-all | bytes 655360 | tf_op jit(solution)/shard_map/all_to_all | solution.py:573
  57.4 0.7 shard_map.80
  58.1 12.5 %all_to_all.16.recv_ref = bf16[16,56,128]{2,1,0:T(8,128)(2,1)S(1)} all-to-all(bf16[16,56,128]{2,1,0:T(8,128)(2,1)S(1)} %get-tuple-element.11), channel_id=1, replica_groups=mesh['peer'=2,'depth'=4,'row'=4] {'depth','row'}, dimensions={0} | all-to-all | bytes 458752 | tf_op jit(solution)/shard_map/all_to_all | solution.py:579
  70.6 0.8 %shard_map.81 = (f32[1,4,32,864]{3,2,1,0:T(8,128)}, f32[1,32,104]{2,1,0:T(8,128)}) custom-call(bf16[16,56,128]{2,1,0:T(8,128)(2,1)S(1)} %all_to_all.16.recv_ref), custom_call_target="tpu_custom_call" | custom-call | tf_op jit(solution)/shard_map/pallas_call | solution.py:580
  (1 shorter events, 0.0 us)
Async XLA Ops:
  0.6 9.3 %copy-start.3 = (bf16[1,4,864,32]{2,3,1,0:T(8,128)(2,1)S(1)}, bf16[1,4,864,32]{2,3,1,0:T(8,128)(2,1)}, u32[]{:S(2)}) copy-start(bf16[1,4,864,32]{2,3,1,0:T(8,128)(2,1)} %param.7) | copy-start | bytes 663556
  0.6 10.9 %copy-start.4 = (bf16[1,32,104]{2,1,0:T(8,128)(2,1)S(1)}, bf16[1,32,104]{2,1,0:T(8,128)(2,1)}, u32[]{:S(2)}) copy-start(bf16[1,32,104]{2,1,0:T(8,128)(2,1)} %param.8) | copy-start | bytes 19972
  2.6 21.9 %all-to-all-start = ((bf16[16,128,128]{2,1,0:T(8,128)(2,1)}), bf16[16,128,128]{2,1,0:T(8,128)(2,1)S(1)}, u32[]{:S(2)}, u32[]{:S(2)}) async-start(bf16[16,128,128]{2,1,0:T(8,128)(2,1)} %shard_map.76), calls=%async_computation | async-start | bytes 1048576 | tf_op jit(solution)/shard_map/all_to_all | solution.py:541
  10.0 8.1 %collective-permute-start = (bf16[1,4,32,864]{3,2,1,0:T(8,128)(2,1)S(1)}, bf16[1,4,32,864]{3,2,1,0:T(8,128)(2,1)S(1)}, u32[]{:S(2)}, u32[]{:S(2)}) collective-permute-start(bf16[1,4,32,864]{3,2,1,0:T(8,128)(2,1)S(1)} %bitcast.6), channel_id=1, source_target_pairs={{0,16},{16,0},{1,17},{17,1},{2,18},{18,2},{3,19},{19,3},{4,20},{20... | collective-permute-start | bytes 663560 | tf_op jit(solution)/shard_map/ppermute | solution.py:519
  11.6 9.0 %collective-permute-start.1 = (bf16[1,32,128]{2,1,0:T(8,128)(2,1)S(1)}, bf16[1,32,128]{2,1,0:T(8,128)(2,1)S(1)}, u32[]{:S(2)}, u32[]{:S(2)}) collective-permute-start(bf16[1,32,128]{2,1,0:T(8,128)(2,1)S(1)} %get-tuple-element.15), channel_id=1, source_target_pairs={{0,16},{16,0},{1,17},{17,1},{2,18},{18,2},{3,19},{19,3},{4,20},{20... | collective-permute-start | bytes 24584 | tf_op jit(solution)/shard_map/ppermute | solution.py:519
  14.3 1.2 %copy-start = (bf16[1,4,2,384,256]{4,3,2,1,0:T(8,128)(2,1)}, bf16[1,4,2,384,256]{4,3,2,1,0:T(8,128)(2,1)S(1)}, u32[]{:S(2)}) copy-start(bf16[1,4,2,384,256]{4,3,2,1,0:T(8,128)(2,1)S(1)} %get-tuple-element.9.band_hbm) | copy-start | bytes 4718596
  15.4 3.9 %copy-start.1 = (bf16[1,4,2,384,256]{4,3,2,1,0:T(8,128)(2,1)}, bf16[1,4,2,384,256]{4,3,2,1,0:T(8,128)(2,1)S(1)}, u32[]{:S(2)}) copy-start(bf16[1,4,2,384,256]{4,3,2,1,0:T(8,128)(2,1)S(1)} %get-tuple-element.10.back_hbm) | copy-start | bytes 4718596
  19.4 1.1 %copy-start.2 = (bf16[1,4,2,384,256]{4,3,2,1,0:T(8,128)(2,1)}, bf16[1,4,2,384,256]{4,3,2,1,0:T(8,128)(2,1)S(1)}, u32[]{:S(2)}) copy-start(bf16[1,4,2,384,256]{4,3,2,1,0:T(8,128)(2,1)S(1)} %shard_map.78.other_hbm) | copy-start | bytes 4718596
where the time goes:
time: 71.7 us; the launch traced here: 71.4 us
  blocking collectives  27.5 us (38%)
  Pallas kernels  24.7 us (34%)
  starting transfers between devices  9.55 us (13%)
  waiting for transfers between devices  6.56 us (9%)
  local copies, waits for them, and re-layouts  2.32 us (3%)
  between operations  0.73 us (1%)
    pallas_call x1, Pallas kernels, body(): call(main_kernel, plan, shape((n, plan.back_rows, LANES), BF16), [pltpu.V...  17.9 us
    all_to_all x1, blocking collectives, body(): parts = lax.all_to_all(parts, GROUP, 0, 0, tiled=True)  15 us
    all_to_all x1, blocking collectives, body(): sums = lax.all_to_all(sums, GROUP, 0, 0, tiled=True)  12.5 us
    all_to_all x1, starting transfers between devices, body(): slabs = lax.all_to_all(packed, GROUP, 0, 0, tiled=True)  7.4 us
    all_to_all x1, waiting for transfers between devices, body(): slabs = lax.all_to_all(packed, GROUP, 0, 0, tiled=True)  3.93 us
    pallas_call x2, Pallas kernels, make_bands(): call(lambda plan, *refs: band_kernel(plan, peers, backward, *refs), plan,...  3.38 us
    ppermute x2, waiting for transfers between devices, from_others(): lax.ppermute(array, 'peer', [(i, (i + q) % peers) for i in range(peers)])  2.63 us
    unnamed x10, local copies, waits for them, and re-layouts  2.31 us
  transfers between devices with their start and end apart: 3, of which 2 were waited for; matrix products, arithmetic and copies ran while one was open for 0% of the time, Pallas kernels for 5%

commit v1 on v0

--- a/solution.py
+++ b/solution.py
@@ -12,6 +12,8 @@
 F32 = jnp.float32
 BF16 = jnp.bfloat16
 GROUP = ("depth", "row")
+MAIN_MIB = 40
+CHUNKS = 3
 
 
 def round_up(value, step):
@@ -74,24 +76,29 @@
         xs[t, at, :] = jnp.where(first_half(), xs[t + 1, at, :], xs[t - 1, at, :])
 
 
-def convolve(xs, slots, matrix, plan):
-    m, rows = plan.m, plan.rows
-    row = lax.rem(lax.broadcasted_iota(jnp.int32, (m, 1), 0), rows)
-    parts = []
-    for half, slot in enumerate(slots):
-        if slot is None:
-            parts.append(None)
-            continue
-        lhs = jnp.concatenate([xs[slot, i * rows : i * rows + m, :] for i in range(3)], axis=1)
-        parts.append(jnp.dot(lhs, matrix(half), preferred_element_type=F32))
-    left, right = (parts[0] if parts[0] is not None else parts[1]), (parts[1] if parts[1] is not None else parts[0])
+def convolve(xs, slots, matrix, plan, use):
+    rows = plan.rows
     mask = first_half()
-    center = jnp.where(mask, left[:, :LANES], right[:, :LANES])
-    before = pltpu.roll(jnp.where(mask, right[:, :LANES], left[:, :LANES]), LANES // 2, 1)
-    after = jnp.where(mask, left[:, LANES:], right[:, LANES:])
-    before = jnp.where(row == 0, 0.0, pltpu.roll(before, 1, 0))
-    after = jnp.where(row == rows - 1, 0.0, pltpu.roll(after, m - 1, 0))
-    return before + center + after
+    step = plan.m // CHUNKS
+    row = lax.rem(lax.broadcasted_iota(jnp.int32, (step, 1), 0), rows)
+    for c in range(CHUNKS):
+        parts = []
+        for half, slot in enumerate(slots):
+            if slot is None:
+                parts.append(None)
+                continue
+            low = c * step
+            lhs = jnp.concatenate([xs[slot, i * rows + low : i * rows + low + step, :] for i in range(3)], axis=1)
+            rhs = jnp.concatenate([matrix(half), matrix(2)], axis=1)
+            parts.append(jnp.dot(lhs, rhs, preferred_element_type=F32))
+        left = parts[0] if parts[0] is not None else parts[1]
+        right = parts[1] if parts[1] is not None else parts[0]
+        center = jnp.where(mask, left[:, :LANES], right[:, :LANES])
+        before = pltpu.roll(jnp.where(mask, right[:, :LANES], left[:, :LANES]), LANES // 2, 1)
+        after = jnp.where(mask, left[:, LANES:], right[:, LANES:])
+        before = jnp.where(row == 0, 0.0, pltpu.roll(before, 1, 0))
+        after = jnp.where(row == rows - 1, 0.0, pltpu.roll(after, step - 1, 0))
+        use(before + center + after, slice(c * step, c * step + step))
 
 
 SLOTS = ({1: 0, 0: 2, 2: 4}, {0: 0, 1: 2, 2: 6})
@@ -143,17 +150,17 @@
                     tall[layer, q * group + u] = part[:, u * PAIR : (u + 1) * PAIR]
 
         def one(layer, carry, peer=peer):
-            for half in range(2):
+            for out, ahead, term in (
+                (outs[0], True, lambda n: wide[layer, n * ch : (n + 1) * ch, :]),
+                (outs[-1], False, lambda n: tall[layer, n]),
+            )[: len(outs)]:
                 for i in range(3):
                     for p in range(group):
                         at = slice((i * group + p) * ch, (i * group + p + 1) * ch)
-                        outs[0][peer, layer, half, at, :] = band_rows(
-                            lambda n: wide[layer, n * ch : (n + 1) * ch, :], True, i, p, half, masks
-                        )
-                        if backward:
-                            outs[1][peer, layer, half, at, :] = band_rows(
-                                lambda n: tall[layer, n], False, i, p, half, masks
-                            )
+                        first, second = [band_rows(term, ahead, i, p, half, masks) for half in range(2)]
+                        out[peer, layer, 0, at, :] = first[:, :LANES]
+                        out[peer, layer, 1, at, :] = second[:, :LANES]
+                        out[peer, layer, 2, at, :] = first[:, LANES:] + second[:, LANES:]
             return carry
 
         lax.fori_loop(0, plan.layers, one, 0)
@@ -244,10 +251,14 @@
         count -= 2
         for b in range(round_up(count, group) // group):
             slots = (2 * b, 2 * b + 1 if b * group + 2 < count else None)
-            total = convolve(source, slots, lambda half: matrix(layer, half), plan)
-            keep(layer, None, b, total)
-            value = total / (1.0 + jnp.exp(-total))
-            target[2 * b, at, :] = jnp.where(crop_mask(b, layer + 1, base, plan), value, 0.0).astype(BF16)
+            inside = crop_mask(b, layer + 1, base, plan)
+
+            def use(total, part, layer=layer, b=b, inside=inside, target=target):
+                keep(layer, None, b, total, part)
+                value = total / (1.0 + jnp.exp(-total))
+                target[2 * b, rows + part.start : rows + part.stop, :] = jnp.where(inside, value, 0.0).astype(BF16)
+
+            convolve(source, slots, lambda half: matrix(layer, half), plan, use)
         source = target
     return source
 
@@ -271,17 +282,11 @@
     return probs
 
 
-def main_kernel(plan, recv_ref, band_hbm, back_hbm, other_hbm, head_ref, heads_ref, out_ref, *scratch):
-    slabs, one_xs, two_xs, acts, pres, label_ref, part, dlog, grads, band, back_band, other_band, sems = scratch
+def main_kernel(plan, recv_ref, band, back_band, other_band, head_ref, heads_ref, out_ref, *scratch):
+    slabs, one_xs, two_xs, acts, pres, label_ref, part, dlog, grads, result = scratch
     ch, m, rows, group, own, layers = plan.channels, plan.m, plan.rows, plan.group, plan.own, plan.layers
     base = position(plan) * own - plan.halo
     peer = lax.axis_index("peer")
-    copies = [pltpu.make_async_copy(band_hbm.at[0, n], band.at[n], sems.at[n]) for n in range(layers)]
-    copies.append(pltpu.make_async_copy(back_hbm.at[0], back_band, sems.at[layers]))
-    first = pltpu.make_async_copy(other_hbm.at[0], other_band, sems.at[layers + 1])
-    for copy in copies:
-        copy.start()
-    first.start()
     buffers = (slabs, one_xs, two_xs)
     for xs in buffers:
         clear_edges(xs, plan)
@@ -290,18 +295,17 @@
     lane = lax.broadcasted_iota(jnp.int32, (1, LANES), 1)
     half_mask = first_half()
 
-    def keep(layer, source, b=None, total=None):
+    def keep(layer, source, b=None, total=None, part=None):
         if source is not None:
-            copies[layer].wait()
             if layer == 0:
                 acts[0, :, 0:LANES] = jnp.where(half_mask, source[6, at, :], source[2, at, :])
             else:
                 acts[layer, :, 0:LANES] = source[2, at, :]
             acts[layer, :, LANES:PAIR] = source[4, at, :]
         elif b < plan.top_blocks:
-            pres[layer, b] = total.astype(BF16)
-
-    last = forward(plan, buffers, 0, lambda layer, half: band[layer, half], base, keep)
+            pres[layer, b, part, :] = total.astype(BF16)
+
+    last = forward(plan, buffers, 0, lambda layer, half: band[0, layer, half], base, keep)
     own_matrix = head_matrix(head_ref[...], plan)
     ones = class_ones(plan)
     pair_lane = lax.rem(lax.broadcasted_iota(jnp.int32, (1, PAIR), 1), LANES).astype(F32)
@@ -323,16 +327,8 @@
     hidden = last[2, at, :]
 
     def other(q, carry):
-        if plan.n_peer > 2:
-
-            @pl.when(q > 0)
-            def fetch():
-                copy = pltpu.make_async_copy(other_hbm.at[q], other_band, sems.at[layers + 2])
-                copy.start()
-                copy.wait()
-
         owner = lax.rem(peer - q - 1 + plan.n_peer, plan.n_peer)
-        last = forward(plan, buffers, 0, lambda layer, half: other_band[layer, half], base, lambda *unused: None)
+        last = forward(plan, buffers, 0, lambda layer, half: other_band[q, layer, half], base, lambda *unused: None)
         matrix = head_matrix(heads_ref[q], plan)
         weight = jnp.where(match == owner.astype(F32), 0.5, 0.0)
         for g in range(3):
@@ -341,7 +337,6 @@
                 part[:, cols] = part[:, cols] - weight * value.astype(BF16).astype(F32)
         return carry
 
-    first.wait()
     if plan.n_peer == 2:
         other(0, 0)
     else:
@@ -370,7 +365,6 @@
 
     row = lax.rem(lax.broadcasted_iota(jnp.int32, (m, 1), 0), rows)
     wide_lane = lax.broadcasted_iota(jnp.int32, (1, PAIR), 1)
-    copies[layers].wait()
     for layer in reversed(range(layers)):
         u = plan.halo - layer - 1
         place = lax.rem(lane // ch - u % group + group, group)
@@ -415,12 +409,16 @@
         fill_odd(level, [t for t in range(start // 2 - 1, plan.top // 2 - 1) if t % 2], plan)
         for b in range(start // group, plan.top_blocks):
             slots = (2 * b - 1 if b * group >= start else None, 2 * b)
-            total = convolve(level, slots, lambda half: back_band[layer, half], plan)
-            if layer > 0:
-                total = total * slope(pres[layer - 1, b])
-                target[2 * b, at, :] = jnp.where(crop_mask(b, layer, base, plan), total, 0.0).astype(BF16)
-            else:
-                result = total
+            inside = crop_mask(b, layer, base, plan)
+
+            def use(total, chunk, layer=layer, b=b, inside=inside, target=target):
+                if layer > 0:
+                    value = jnp.where(inside, total * slope(pres[layer - 1, b, chunk, :]), 0.0)
+                    target[2 * b, rows + chunk.start : rows + chunk.stop, :] = value.astype(BF16)
+                else:
+                    result[chunk, :] = total
+
+            convolve(level, slots, lambda half: back_band[0, layer, half], plan, use)
         level = target
 
     for d in range(plan.n_depth):
@@ -501,7 +499,7 @@
 
 def make_bands(plan, turned, backward):
     peers = turned.shape[0]
-    shape = jax.ShapeDtypeStruct((peers, plan.layers, 2, 3 * LANES, PAIR), BF16)
+    shape = jax.ShapeDtypeStruct((peers, plan.layers, 3, 3 * LANES, LANES), BF16)
     made = call(
         lambda plan, *refs: band_kernel(plan, peers, backward, *refs),
         plan,
@@ -512,7 +510,7 @@
         ],
         cost=pl.CostEstimate(flops=10**9, bytes_accessed=4 * 10**6, transcendentals=0),
     )(turned)
-    return [hbm(x) for x in made]
+    return made
 
 
 def from_others(array, peers):
@@ -547,7 +545,6 @@
     padded = m + 2 * plan.rows
     wide = 3 * plan.group * LANES
     windows = 2 * plan.blocks
-    banded = pltpu.VMEM((layers, 2, 3 * LANES, PAIR), BF16)
     parts = call(
         main_kernel,
         plan,
@@ -562,13 +559,10 @@
             pltpu.VMEM((m, wide), F32),
             pltpu.VMEM((m, wide), BF16),
             pltpu.VMEM((n * plan.chunk, LANES), F32),
-            banded,
-            banded,
-            banded,
-            pltpu.SemaphoreType.DMA((layers + 3,)),
+            pltpu.VMEM((m, LANES), F32),
         ],
-        specs=(True, False, False, False, True, True),
-        limit=48,
+        specs=(True,) * 6,
+        limit=MAIN_MIB,
     )(slabs, band, back_band, other_band, head[0], heads)
     parts = lax.all_to_all(parts, GROUP, 0, 0, tiled=True)
     sums, input_grads = call(

time: 71.7 us -> 69.9 us (0.975)
  Pallas kernels: 24.7 us -> 21.9 us
  waiting for transfers between devices: 6.56 us -> 7.53 us
    pallas_call x1, Pallas kernels: 17.9 us -> 14.8 us  [body(): call(main_kernel, plan, shape((n, plan.back_rows, LANES), BF16), [pltpu.V...]
    ppermute x2, waiting for transfers between devices: 2.63 us -> 3.59 us  [from_others(): lax.ppermute(array, 'peer', [(i, (i + q) % peers) for i in range(peers)])]
    unnamed x10 -> x8, local copies, waits for them, and re-layouts: 2.31 us -> 2.29 us
where the time goes in v1:
time: 69.9 us; the launch traced here: 69.5 us
  blocking collectives  27.6 us (39%)
  Pallas kernels  21.9 us (31%)
  starting transfers between devices  9.55 us (14%)
  waiting for transfers between devices  7.53 us (11%)
  local copies, waits for them, and re-layouts  2.3 us (3%)
  between operations  0.71 us (1%)
    all_to_all x1, blocking collectives, body(): parts = lax.all_to_all(parts, GROUP, 0, 0, tiled=True)  15 us
    pallas_call x1, Pallas kernels, body(): call(main_kernel, plan, shape((n, plan.back_rows, LANES), BF16), [pltpu.V...  14.8 us
    all_to_all x1, blocking collectives, body(): sums = lax.all_to_all(sums, GROUP, 0, 0, tiled=True)  12.5 us
    all_to_all x1, starting transfers between devices, body(): slabs = lax.all_to_all(packed, GROUP, 0, 0, tiled=True)  7.4 us
    all_to_all x1, waiting for transfers between devices, body(): slabs = lax.all_to_all(packed, GROUP, 0, 0, tiled=True)  3.94 us
    pallas_call x2, Pallas kernels, make_bands(): call(lambda plan, *refs: band_kernel(plan, peers, backward, *refs), plan,...  3.73 us
    ppermute x2, waiting for transfers between devices, from_others(): lax.ppermute(array, 'peer', [(i, (i + q) % peers) for i in range(peers)])  3.59 us
    unnamed x8, local copies, waits for them, and re-layouts  2.29 us
  transfers between devices with their start and end apart: 3, of which 2 were waited for; matrix products, arithmetic and copies ran while one was open for 0% of the time, Pallas kernels for 5%

profile of v1, /device:TPU:0, one launch (start us, length us, event | category | flops | bytes accessed | tf_op | source)
XLA Modules:
  0.0 69.5 jit_solution(11903226022945062660)
XLA Ops:
  0.6 0.0 copy-start.2
  0.6 0.0 copy-start.3
  0.7 1.9 %shard_map.76 = bf16[16,128,128]{2,1,0:T(8,128)(2,1)} custom-call(s32[2,3]{1,0:T(2,128)} %bitcast.8, bf16[3,8,2048]{2,1,0:T(8,128)(2,1)} %feat_hbm.1, s32[3,8,64]{2,1,0:T(8,128)} %label_hbm.1), custom_call_target="tpu_custom_call" | custom-call | tf_op jit(solution)/shard_map/pallas_call | solution.py:527
  2.6 7.4 %all-to-all-start = ((bf16[16,128,128]{2,1,0:T(8,128)(2,1)}), bf16[16,128,128]{2,1,0:T(8,128)(2,1)S(1)}, u32[]{:S(2)}, u32[]{:S(2)}) async-start(bf16[16,128,128]{2,1,0:T(8,128)(2,1)} %shard_map.76), calls=%async_computation | async-start | bytes 1048576 | tf_op jit(solution)/shard_map/all_to_all | solution.py:539
  10.0 0.0 copy-done.2
  10.0 1.6 %collective-permute-start = (bf16[1,4,32,864]{3,2,1,0:T(8,128)(2,1)S(1)}, bf16[1,4,32,864]{3,2,1,0:T(8,128)(2,1)S(1)}, u32[]{:S(2)}, u32[]{:S(2)}) collective-permute-start(bf16[1,4,32,864]{3,2,1,0:T(8,128)(2,1)S(1)} %bitcast.6), channel_id=1, source_target_pairs={{0,16},{16,0},{1,17},{17,1},{2,18},{18,2},{3,19},{19,3},{4,20},{20... | collective-permute-start | bytes 663560 | tf_op jit(solution)/shard_map/ppermute | solution.py:517
  11.6 0.0 copy-done.3
  11.6 0.6 collective-permute-start.1
  12.2 2.3 %shard_map.77 = (bf16[1,4,3,384,128]{4,3,2,1,0:T(8,128)(2,1)S(1)}, bf16[1,4,3,384,128]{4,3,2,1,0:T(8,128)(2,1)S(1)}) custom-call(bf16[1,4,32,864]{3,2,1,0:T(8,128)(2,1)S(1)} %bitcast.7), custom_call_target="tpu_custom_call" | custom-call | flops 1000000000 | bytes 4000000 | tf_op jit(solution)/shard_map/pallas_call | solution.py:503
  14.5 3.6 %collective-permute-done.refs_0_ = bf16[1,4,32,864]{3,2,1,0:T(8,128)(2,1)S(1)} collective-permute-done((bf16[1,4,32,864]{3,2,1,0:T(8,128)(2,1)S(1)}, bf16[1,4,32,864]{3,2,1,0:T(8,128)(2,1)S(1)}, u32[]{:S(2)}, u32[]{:S(2)}) %collective-permute-start) | collective-permute-done | bytes 221216 | tf_op jit(solution)/shard_map/ppermute | solution.py:517
  18.1 1.4 %shard_map.78.other_band = bf16[1,4,3,384,128]{4,3,2,1,0:T(8,128)(2,1)S(1)} custom-call(bf16[1,4,32,864]{3,2,1,0:T(8,128)(2,1)S(1)} %collective-permute-done.refs_0_), custom_call_target="tpu_custom_call" | custom-call | flops 1000000000 | bytes 4000000 | tf_op jit(solution)/shard_map/pallas_call | solution.py:503
  19.5 0.0 copy-start
  19.5 1.0 %copy-done = bf16[1,4,3,384,128]{4,3,2,1,0:T(8,128)(2,1)} copy-done((bf16[1,4,3,384,128]{4,3,2,1,0:T(8,128)(2,1)}, bf16[1,4,3,384,128]{4,3,2,1,0:T(8,128)(2,1)S(1)}, u32[]{:S(2)}) %copy-start) | copy-done | bytes 1179672
  20.5 0.0 collective-permute-done.1.heads_ref
  20.5 3.9 %all-to-all-done.recv_ref = bf16[16,128,128]{2,1,0:T(8,128)(2,1)S(1)} async-done(((bf16[16,128,128]{2,1,0:T(8,128)(2,1)}), bf16[16,128,128]{2,1,0:T(8,128)(2,1)S(1)}, u32[]{:S(2)}, u32[]{:S(2)}) %all-to-all-start) | async-done | bytes 524320 | tf_op jit(solution)/shard_map/all_to_all | solution.py:539
  24.5 0.0 copy-start.1
  24.5 1.3 %copy-done.1 = bf16[1,4,3,384,128]{4,3,2,1,0:T(8,128)(2,1)S(1)} copy-done((bf16[1,4,3,384,128]{4,3,2,1,0:T(8,128)(2,1)S(1)}, bf16[1,4,3,384,128]{4,3,2,1,0:T(8,128)(2,1)}, u32[]{:S(2)}) %copy-start.1) | copy-done | bytes 1179672
  25.7 14.8 %shard_map.79 = bf16[16,80,128]{2,1,0:T(8,128)(2,1)S(1)} custom-call(bf16[16,128,128]{2,1,0:T(8,128)(2,1)S(1)} %all-to-all-done.recv_ref, bf16[1,4,3,384,128]{4,3,2,1,0:T(8,128)(2,1)S(1)} %get-tuple-element.9.band, bf16[1,4,3,384,128]{4,3,2,1,0:T(8,128)(2,1)S(1)} %get-tuple-element.10.back_band, bf16[1,4,3,384,128]{4,3,2,1,0:T(8,128)(2,1)S(1)} %copy-done.1, ...), custom_call_target="tpu_custom_call" | custom-call | tf_op jit(solution)/shard_map/pallas_call | solution.py:548
  40.5 15.0 %all_to_all.15.recv_ref = bf16[16,80,128]{2,1,0:T(8,128)(2,1)S(1)} all-to-all(bf16[16,80,128]{2,1,0:T(8,128)(2,1)S(1)} %shard_map.79), channel_id=1, replica_groups=mesh['peer'=2,'depth'=4,'row'=4] {'depth','row'}, dimensions={0} | all-to-all | bytes 655360 | tf_op jit(solution)/shard_map/all_to_all | solution.py:567
  55.5 0.7 shard_map.80
  56.2 12.5 %all_to_all.16.recv_ref = bf16[16,56,128]{2,1,0:T(8,128)(2,1)S(1)} all-to-all(bf16[16,56,128]{2,1,0:T(8,128)(2,1)S(1)} %get-tuple-element.11), channel_id=1, replica_groups=mesh['peer'=2,'depth'=4,'row'=4] {'depth','row'}, dimensions={0} | all-to-all | bytes 458752 | tf_op jit(solution)/shard_map/all_to_all | solution.py:573
  68.7 0.8 %shard_map.81 = (f32[1,4,32,864]{3,2,1,0:T(8,128)}, f32[1,32,104]{2,1,0:T(8,128)}) custom-call(bf16[16,56,128]{2,1,0:T(8,128)(2,1)S(1)} %all_to_all.16.recv_ref), custom_call_target="tpu_custom_call" | custom-call | tf_op jit(solution)/shard_map/pallas_call | solution.py:574
  (1 shorter events, 0.0 us)
Async XLA Ops:
  0.6 9.4 %copy-start.2 = (bf16[1,4,864,32]{2,3,1,0:T(8,128)(2,1)S(1)}, bf16[1,4,864,32]{2,3,1,0:T(8,128)(2,1)}, u32[]{:S(2)}) copy-start(bf16[1,4,864,32]{2,3,1,0:T(8,128)(2,1)} %param.7) | copy-start | bytes 663556
  0.6 10.9 %copy-start.3 = (bf16[1,32,104]{2,1,0:T(8,128)(2,1)S(1)}, bf16[1,32,104]{2,1,0:T(8,128)(2,1)}, u32[]{:S(2)}) copy-start(bf16[1,32,104]{2,1,0:T(8,128)(2,1)} %param.8) | copy-start | bytes 19972
  2.6 21.9 %all-to-all-start = ((bf16[16,128,128]{2,1,0:T(8,128)(2,1)}), bf16[16,128,128]{2,1,0:T(8,128)(2,1)S(1)}, u32[]{:S(2)}, u32[]{:S(2)}) async-start(bf16[16,128,128]{2,1,0:T(8,128)(2,1)} %shard_map.76), calls=%async_computation | async-start | bytes 1048576 | tf_op jit(solution)/shard_map/all_to_all | solution.py:539
  10.0 8.1 %collective-permute-start = (bf16[1,4,32,864]{3,2,1,0:T(8,128)(2,1)S(1)}, bf16[1,4,32,864]{3,2,1,0:T(8,128)(2,1)S(1)}, u32[]{:S(2)}, u32[]{:S(2)}) collective-permute-start(bf16[1,4,32,864]{3,2,1,0:T(8,128)(2,1)S(1)} %bitcast.6), channel_id=1, source_target_pairs={{0,16},{16,0},{1,17},{17,1},{2,18},{18,2},{3,19},{19,3},{4,20},{20... | collective-permute-start | bytes 663560 | tf_op jit(solution)/shard_map/ppermute | solution.py:517
  11.6 8.9 %collective-permute-start.1 = (bf16[1,32,128]{2,1,0:T(8,128)(2,1)S(1)}, bf16[1,32,128]{2,1,0:T(8,128)(2,1)S(1)}, u32[]{:S(2)}, u32[]{:S(2)}) collective-permute-start(bf16[1,32,128]{2,1,0:T(8,128)(2,1)S(1)} %get-tuple-element.15), channel_id=1, source_target_pairs={{0,16},{16,0},{1,17},{17,1},{2,18},{18,2},{3,19},{19,3},{4,20},{20... | collective-permute-start | bytes 24584 | tf_op jit(solution)/shard_map/ppermute | solution.py:517
  19.5 1.0 %copy-start = (bf16[1,4,3,384,128]{4,3,2,1,0:T(8,128)(2,1)}, bf16[1,4,3,384,128]{4,3,2,1,0:T(8,128)(2,1)S(1)}, u32[]{:S(2)}) copy-start(bf16[1,4,3,384,128]{4,3,2,1,0:T(8,128)(2,1)S(1)} %shard_map.78.other_band) | copy-start | bytes 3538948
  24.5 1.3 %copy-start.1 = (bf16[1,4,3,384,128]{4,3,2,1,0:T(8,128)(2,1)S(1)}, bf16[1,4,3,384,128]{4,3,2,1,0:T(8,128)(2,1)}, u32[]{:S(2)}) copy-start(bf16[1,4,3,384,128]{4,3,2,1,0:T(8,128)(2,1)} %copy-done) | copy-start | bytes 3538948

commit v2 on v1

--- a/solution.py
+++ b/solution.py
@@ -12,7 +12,8 @@
 F32 = jnp.float32
 BF16 = jnp.bfloat16
 GROUP = ("depth", "row")
-MAIN_MIB = 40
+FORWARD_MIB = 32
+BACKWARD_MIB = 24
 CHUNKS = 3
 
 
@@ -239,11 +240,11 @@
                 label_ref[at : at + rows, :] = jnp.where((lane < seen) | (lane == keep), piece, 0.0)
 
 
-def forward(plan, buffers, first, matrix, base, keep):
+def forward_steps(plan, buffers, matrix, base, keep):
     m, rows, group = plan.m, plan.rows, plan.group
     at = slice(rows, rows + m)
     count = plan.window
-    source = buffers[first]
+    source = buffers[0]
     for layer in range(plan.layers):
         target = buffers[1 + layer % 2]
         fill_odd(source, range(1, (count - 4) // 2 + 1, 2), plan)
@@ -259,8 +260,12 @@
                 target[2 * b, rows + part.start : rows + part.stop, :] = jnp.where(inside, value, 0.0).astype(BF16)
 
             convolve(source, slots, lambda half: matrix(layer, half), plan, use)
+            yield
         source = target
-    return source
+
+
+def last_of(buffers, plan):
+    return buffers[1 + (plan.layers - 1) % 2]
 
 
 def class_ones(plan):
@@ -282,18 +287,20 @@
     return probs
 
 
-def main_kernel(plan, recv_ref, band, back_band, other_band, head_ref, heads_ref, out_ref, *scratch):
-    slabs, one_xs, two_xs, acts, pres, label_ref, part, dlog, grads, result = scratch
-    ch, m, rows, group, own, layers = plan.channels, plan.m, plan.rows, plan.group, plan.own, plan.layers
-    base = position(plan) * own - plan.halo
+def forward_kernel(plan, recv_ref, band, other_band, head_ref, heads_ref, acts, pres, dlog, hidden_ref, *scratch):
+    slabs, one_xs, two_xs, three_xs, four_xs, label_ref, part = scratch
+    m, rows, group = plan.m, plan.rows, plan.group
+    base = position(plan) * plan.own - plan.halo
     peer = lax.axis_index("peer")
-    buffers = (slabs, one_xs, two_xs)
-    for xs in buffers:
+    buffers, others = (slabs, one_xs, two_xs), (slabs, three_xs, four_xs)
+    for xs in scratch[:5]:
         clear_edges(xs, plan)
     unpack_slabs(plan, recv_ref, slabs, label_ref)
     at = slice(rows, rows + m)
-    lane = lax.broadcasted_iota(jnp.int32, (1, LANES), 1)
     half_mask = first_half()
+
+    def drop(*unused):
+        pass
 
     def keep(layer, source, b=None, total=None, part=None):
         if source is not None:
@@ -305,7 +312,17 @@
         elif b < plan.top_blocks:
             pres[layer, b, part, :] = total.astype(BF16)
 
-    last = forward(plan, buffers, 0, lambda layer, half: band[0, layer, half], base, keep)
+    own_steps = forward_steps(plan, buffers, lambda layer, half: band[0, layer, half], base, keep)
+    if plan.n_peer == 2:
+        other_steps = forward_steps(plan, others, lambda layer, half: other_band[0, layer, half], base, drop)
+        for unused in zip(own_steps, other_steps):
+            pass
+        for unused in other_steps:
+            pass
+    else:
+        for unused in own_steps:
+            pass
+    last = last_of(buffers, plan)
     own_matrix = head_matrix(head_ref[...], plan)
     ones = class_ones(plan)
     pair_lane = lax.rem(lax.broadcasted_iota(jnp.int32, (1, PAIR), 1), LANES).astype(F32)
@@ -315,35 +332,61 @@
     codes = labels.astype(BF16)
     match = labels[:, LANES - plan.slab_depth : LANES - plan.slab_depth + 1]
     weight = jnp.where(match == peer.astype(F32), 0.5, 0.0)
-    for g in range(3):
-        for u, value in enumerate(probabilities(last[2 * g, at, :], own_matrix, ones, plan)):
-            place = g * group + 2 * u
-            spread = (spread_r == spread_l + place).astype(BF16)
-            label = jnp.dot(codes, spread, preferred_element_type=F32)
-            onehot = jnp.where(label == pair_lane, 0.5, 0.0)
-            part[:, place * LANES : place * LANES + PAIR] = (
-                value - onehot - weight * value.astype(BF16).astype(F32)
-            )
-    hidden = last[2, at, :]
-
-    def other(q, carry):
+    def minus_targets(g, u, value):
+        place = g * group + 2 * u
+        spread = (spread_r == spread_l + place).astype(BF16)
+        label = jnp.dot(codes, spread, preferred_element_type=F32)
+        onehot = jnp.where(label == pair_lane, 0.5, 0.0)
+        return value - onehot - weight * value.astype(BF16).astype(F32)
+
+    def columns_of(g, u):
+        return slice((g * group + 2 * u) * LANES, (g * group + 2 * u + 2) * LANES)
+
+    def other_share(q, last):
         owner = lax.rem(peer - q - 1 + plan.n_peer, plan.n_peer)
-        last = forward(plan, buffers, 0, lambda layer, half: other_band[q, layer, half], base, lambda *unused: None)
         matrix = head_matrix(heads_ref[q], plan)
         weight = jnp.where(match == owner.astype(F32), 0.5, 0.0)
         for g in range(3):
             for u, value in enumerate(probabilities(last[2 * g, at, :], matrix, ones, plan)):
-                cols = slice((g * group + 2 * u) * LANES, (g * group + 2 * u + 2) * LANES)
-                part[:, cols] = part[:, cols] - weight * value.astype(BF16).astype(F32)
+                yield g, u, weight * value.astype(BF16).astype(F32)
+
+    own_probs = (
+        (g, u, value)
+        for g in range(3)
+        for u, value in enumerate(probabilities(last[2 * g, at, :], own_matrix, ones, plan))
+    )
+    if plan.n_peer == 2:
+        for (g, u, value), (unused, unused, share) in zip(own_probs, other_share(0, last_of(others, plan))):
+            dlog[:, columns_of(g, u)] = (minus_targets(g, u, value) - share).astype(BF16)
+    else:
+        for g, u, value in own_probs:
+            part[:, columns_of(g, u)] = minus_targets(g, u, value)
+    hidden_ref[...] = last[2, at, :]
+
+    def other(q, carry):
+        for unused in forward_steps(plan, others, lambda layer, half: other_band[q, layer, half], base, drop):
+            pass
+        for g, u, share in other_share(q, last_of(others, plan)):
+            part[:, columns_of(g, u)] = part[:, columns_of(g, u)] - share
         return carry
 
-    if plan.n_peer == 2:
-        other(0, 0)
-    else:
+    if plan.n_peer > 2:
         lax.fori_loop(0, plan.n_peer - 1, other, 0)
+        dlog[...] = part[...].astype(BF16)
+
+
+def backward_kernel(plan, back_band, head_ref, acts, pres, dlog, hidden_ref, out_ref, *scratch):
+    slabs, one_xs, two_xs, grads, result = scratch
+    ch, m, rows, group, own, layers = plan.channels, plan.m, plan.rows, plan.group, plan.own, plan.layers
+    base = position(plan) * own - plan.halo
+    for xs in scratch[:3]:
+        clear_edges(xs, plan)
+    at = slice(rows, rows + m)
+    lane = lax.broadcasted_iota(jnp.int32, (1, LANES), 1)
+    own_matrix = head_matrix(head_ref[...], plan)
+    hidden = hidden_ref[...]
 
     wide = group * LANES
-    dlog[...] = part[...].astype(BF16)
     level = one_xs
     for g in range(3):
         back = lax.dot_general(
@@ -503,7 +546,7 @@
     made = call(
         lambda plan, *refs: band_kernel(plan, peers, backward, *refs),
         plan,
-        [shape] * (2 if backward else 1),
+        [shape, pltpu.HBM(shape.shape, shape.dtype)] if backward else [shape],
         [
             pltpu.VMEM((plan.layers, plan.taps, PAIR), BF16),
             pltpu.VMEM((plan.layers, plan.taps // plan.channels, plan.channels, PAIR), BF16),
@@ -545,25 +588,38 @@
     padded = m + 2 * plan.rows
     wide = 3 * plan.group * LANES
     windows = 2 * plan.blocks
+    kept = call(
+        forward_kernel,
+        plan,
+        [
+            shape((layers, m, PAIR), BF16),
+            shape((layers, plan.top_blocks, m, LANES), BF16),
+            shape((m, wide), BF16),
+            shape((m, LANES), BF16),
+        ],
+        [pltpu.VMEM((windows, padded, LANES), BF16)] * 5
+        + [
+            pltpu.VMEM((m, LANES), F32),
+            pltpu.VMEM((m, wide), F32),
+        ],
+        specs=(True,) * 5,
+        cost=pl.CostEstimate(flops=8 * 10**9, bytes_accessed=10**7, transcendentals=0),
+        limit=FORWARD_MIB,
+    )(slabs, band, other_band, head[0], heads)
     parts = call(
-        main_kernel,
+        backward_kernel,
         plan,
         shape((n, plan.back_rows, LANES), BF16),
         [
-            pltpu.VMEM((windows, padded, LANES), BF16),
-            pltpu.VMEM((windows, padded, LANES), BF16),
-            pltpu.VMEM((windows, padded, LANES), BF16),
-            pltpu.VMEM((layers, m, PAIR), BF16),
-            pltpu.VMEM((layers, plan.top_blocks, m, LANES), BF16),
-            pltpu.VMEM((m, LANES), F32),
-            pltpu.VMEM((m, wide), F32),
-            pltpu.VMEM((m, wide), BF16),
+            pltpu.VMEM((2, padded, LANES), BF16),
+            pltpu.VMEM((2 * plan.top_blocks, padded, LANES), BF16),
+            pltpu.VMEM((2 * plan.top_blocks, padded, LANES), BF16),
             pltpu.VMEM((n * plan.chunk, LANES), F32),
             pltpu.VMEM((m, LANES), F32),
         ],
         specs=(True,) * 6,
-        limit=MAIN_MIB,
-    )(slabs, band, back_band, other_band, head[0], heads)
+        limit=BACKWARD_MIB,
+    )(back_band, head[0], *kept)
     parts = lax.all_to_all(parts, GROUP, 0, 0, tiled=True)
     sums, input_grads = call(
         sum_kernel,

time: 69.9 us -> 68.7 us (0.983)
  local copies, waits for them, and re-layouts: 2.3 us -> 0.02 us
  Pallas kernels: 21.9 us -> 23.1 us
    unnamed x8 -> x6, local copies, waits for them, and re-layouts: 2.29 us -> 0.01 us
    pallas_call x2, Pallas kernels: 3.73 us -> 4.75 us  [make_bands(): call(lambda plan, *refs: band_kernel(plan, peers, backward, *refs), plan,...]
    ppermute x2, waiting for transfers between devices: 3.59 us -> 2.57 us  [from_others(): lax.ppermute(array, 'peer', [(i, (i + q) % peers) for i in range(peers)])]
    all_to_all x1, waiting for transfers between devices: 3.94 us -> 4.95 us  [body(): slabs = lax.all_to_all(packed, GROUP, 0, 0, tiled=True)]
    pallas_call x1 -> x2, Pallas kernels: 14.8 us -> 14.9 us  [the longest x1 10.3 us: body(): call(forward_kernel, plan, [shape((layers, m, PAIR), BF16), shape((layers...]
  transfers between devices with their start and end apart: 3 -> 3, of which waited for: 2 -> 2; matrix products, arithmetic and copies ran while one was open for 0% -> 0% of each run, Pallas kernels for 5% -> 7%
where the time goes in v2:
time: 68.7 us; the launch traced here: 68.4 us
  blocking collectives  27.6 us (40%)
  Pallas kernels  23.1 us (34%)
  starting transfers between devices  9.55 us (14%)
  waiting for transfers between devices  7.52 us (11%)
  between operations  0.72 us (1%)
    all_to_all x1, blocking collectives, body(): parts = lax.all_to_all(parts, GROUP, 0, 0, tiled=True)  15 us
    all_to_all x1, blocking collectives, body(): sums = lax.all_to_all(sums, GROUP, 0, 0, tiled=True)  12.5 us
    pallas_call x1, Pallas kernels, body(): call(forward_kernel, plan, [shape((layers, m, PAIR), BF16), shape((layers...  10.3 us
    all_to_all x1, starting transfers between devices, body(): slabs = lax.all_to_all(packed, GROUP, 0, 0, tiled=True)  7.4 us
    all_to_all x1, waiting for transfers between devices, body(): slabs = lax.all_to_all(packed, GROUP, 0, 0, tiled=True)  4.95 us
    pallas_call x2, Pallas kernels, make_bands(): call(lambda plan, *refs: band_kernel(plan, peers, backward, *refs), plan,...  4.75 us
    pallas_call x1, Pallas kernels, body(): call(backward_kernel, plan, shape((n, plan.back_rows, LANES), BF16), [plt...  4.63 us
    ppermute x2, waiting for transfers between devices, from_others(): lax.ppermute(array, 'peer', [(i, (i + q) % peers) for i in range(peers)])  2.57 us
  transfers between devices with their start and end apart: 3, of which 2 were waited for; matrix products, arithmetic and copies ran while one was open for 0% of the time, Pallas kernels for 7%

profile of v2, /device:TPU:0, one launch (start us, length us, event | category | flops | bytes accessed | tf_op | source)
XLA Modules:
  0.0 68.4 jit_solution(13984050243499031451)
XLA Ops:
  0.6 0.0 copy-start.1
  0.6 0.0 copy-start.2
  0.7 1.9 %shard_map.77 = bf16[16,128,128]{2,1,0:T(8,128)(2,1)} custom-call(s32[2,3]{1,0:T(2,128)} %bitcast.8, bf16[3,8,2048]{2,1,0:T(8,128)(2,1)} %feat_hbm.1, s32[3,8,64]{2,1,0:T(8,128)} %label_hbm.1), custom_call_target="tpu_custom_call" | custom-call | tf_op jit(solution)/shard_map/pallas_call | solution.py:570
  2.6 7.4 %all-to-all-start = ((bf16[16,128,128]{2,1,0:T(8,128)(2,1)}), bf16[16,128,128]{2,1,0:T(8,128)(2,1)S(1)}, u32[]{:S(2)}, u32[]{:S(2)}) async-start(bf16[16,128,128]{2,1,0:T(8,128)(2,1)} %shard_map.77), calls=%async_computation | async-start | bytes 1048576 | tf_op jit(solution)/shard_map/all_to_all | solution.py:582
  10.0 0.0 copy-done.1
  10.0 1.6 %collective-permute-start = (bf16[1,4,32,864]{3,2,1,0:T(8,128)(2,1)S(1)}, bf16[1,4,32,864]{3,2,1,0:T(8,128)(2,1)S(1)}, u32[]{:S(2)}, u32[]{:S(2)}) collective-permute-start(bf16[1,4,32,864]{3,2,1,0:T(8,128)(2,1)S(1)} %bitcast.6), channel_id=1, source_target_pairs={{0,16},{16,0},{1,17},{17,1},{2,18},{18,2},{3,19},{19,3},{4,20},{20... | collective-permute-start | bytes 663560 | tf_op jit(solution)/shard_map/ppermute | solution.py:560
  11.6 0.0 copy-done.2
  11.6 0.6 collective-permute-start.1
  12.2 3.4 %shard_map.76 = (bf16[1,4,3,384,128]{4,3,2,1,0:T(8,128)(2,1)S(1)}, bf16[1,4,3,384,128]{4,3,2,1,0:T(8,128)(2,1)}) custom-call(bf16[1,4,32,864]{3,2,1,0:T(8,128)(2,1)S(1)} %bitcast.7), custom_call_target="tpu_custom_call" | custom-call | flops 1000000000 | bytes 4000000 | tf_op jit(solution)/shard_map/pallas_call | solution.py:546
  15.5 2.6 %collective-permute-done.refs_0_ = bf16[1,4,32,864]{3,2,1,0:T(8,128)(2,1)S(1)} collective-permute-done((bf16[1,4,32,864]{3,2,1,0:T(8,128)(2,1)S(1)}, bf16[1,4,32,864]{3,2,1,0:T(8,128)(2,1)S(1)}, u32[]{:S(2)}, u32[]{:S(2)}) %collective-permute-start) | collective-permute-done | bytes 221216 | tf_op jit(solution)/shard_map/ppermute | solution.py:560
  18.1 1.4 %shard_map.78.other_band = bf16[1,4,3,384,128]{4,3,2,1,0:T(8,128)(2,1)S(1)} custom-call(bf16[1,4,32,864]{3,2,1,0:T(8,128)(2,1)S(1)} %collective-permute-done.refs_0_), custom_call_target="tpu_custom_call" | custom-call | flops 1000000000 | bytes 4000000 | tf_op jit(solution)/shard_map/pallas_call | solution.py:546
  19.5 0.0 collective-permute-done.1.heads_ref
  19.5 5.0 %all-to-all-done.recv_ref = bf16[16,128,128]{2,1,0:T(8,128)(2,1)S(1)} async-done(((bf16[16,128,128]{2,1,0:T(8,128)(2,1)}), bf16[16,128,128]{2,1,0:T(8,128)(2,1)S(1)}, u32[]{:S(2)}, u32[]{:S(2)}) %all-to-all-start) | async-done | bytes 524320 | tf_op jit(solution)/shard_map/all_to_all | solution.py:582
  24.5 0.0 copy-start
  24.5 10.3 %shard_map.79 = (bf16[4,384,256]{2,1,0:T(8,128)(2,1)S(1)}, bf16[4,3,384,128]{3,2,1,0:T(8,128)(2,1)S(1)}, bf16[384,1536]{1,0:T(8,128)(2,1)S(1)}, bf16[384,128]{1,0:T(8,128)(2,1)S(1)}) custom-call(bf16[16,128,128]{2,1,0:T(8,128)(2,1)S(1)} %all-to-all-done.recv_ref, bf16[1,4,3,384,128]{4,3,2,1,0:T(8,128)(2,1)S(1)} %get-tuple-element.14.band, ...), custom_call_target="tpu_custom_call" | custom-call | flops 8000000000 | bytes 10000000 | tf_op jit(solution)/shard_map/pallas_call | solution.py:591
  34.8 0.0 copy-done
  34.8 4.6 %shard_map.80 = bf16[16,80,128]{2,1,0:T(8,128)(2,1)S(1)} custom-call(bf16[1,4,3,384,128]{4,3,2,1,0:T(8,128)(2,1)S(1)} %copy-done, bf16[32,128]{1,0:T(8,128)(2,1)S(1)} %get-tuple-element.24.head_ref, bf16[4,384,256]{2,1,0:T(8,128)(2,1)S(1)} %get-tuple-element.15.acts, bf16[4,3,384,128]{3,2,1,0:T(8,128)(2,1)S(1)} %get-tuple-element.16.pres, ...), custom_call_target="tpu_custom_call" | custom-call | tf_op jit(solution)/shard_map/pallas_call | solution.py:609
  39.4 15.0 %all_to_all.15.recv_ref = bf16[16,80,128]{2,1,0:T(8,128)(2,1)S(1)} all-to-all(bf16[16,80,128]{2,1,0:T(8,128)(2,1)S(1)} %shard_map.80), channel_id=1, replica_groups=mesh['peer'=2,'depth'=4,'row'=4] {'depth','row'}, dimensions={0} | all-to-all | bytes 655360 | tf_op jit(solution)/shard_map/all_to_all | solution.py:623
  54.4 0.7 shard_map.81
  55.1 12.5 %all_to_all.16.recv_ref = bf16[16,56,128]{2,1,0:T(8,128)(2,1)S(1)} all-to-all(bf16[16,56,128]{2,1,0:T(8,128)(2,1)S(1)} %get-tuple-element.19), channel_id=1, replica_groups=mesh['peer'=2,'depth'=4,'row'=4] {'depth','row'}, dimensions={0} | all-to-all | bytes 458752 | tf_op jit(solution)/shard_map/all_to_all | solution.py:629
  67.6 0.8 %shard_map.82 = (f32[1,4,32,864]{3,2,1,0:T(8,128)}, f32[1,32,104]{2,1,0:T(8,128)}) custom-call(bf16[16,56,128]{2,1,0:T(8,128)(2,1)S(1)} %all_to_all.16.recv_ref), custom_call_target="tpu_custom_call" | custom-call | tf_op jit(solution)/shard_map/pallas_call | solution.py:630
  (1 shorter events, 0.0 us)
Async XLA Ops:
  0.6 9.4 %copy-start.1 = (bf16[1,4,864,32]{2,3,1,0:T(8,128)(2,1)S(1)}, bf16[1,4,864,32]{2,3,1,0:T(8,128)(2,1)}, u32[]{:S(2)}) copy-start(bf16[1,4,864,32]{2,3,1,0:T(8,128)(2,1)} %param.7) | copy-start | bytes 663556
  0.6 10.9 %copy-start.2 = (bf16[1,32,104]{2,1,0:T(8,128)(2,1)S(1)}, bf16[1,32,104]{2,1,0:T(8,128)(2,1)}, u32[]{:S(2)}) copy-start(bf16[1,32,104]{2,1,0:T(8,128)(2,1)} %param.8) | copy-start | bytes 19972
  2.6 21.9 %all-to-all-start = ((bf16[16,128,128]{2,1,0:T(8,128)(2,1)}), bf16[16,128,128]{2,1,0:T(8,128)(2,1)S(1)}, u32[]{:S(2)}, u32[]{:S(2)}) async-start(bf16[16,128,128]{2,1,0:T(8,128)(2,1)} %shard_map.77), calls=%async_computation | async-start | bytes 1048576 | tf_op jit(solution)/shard_map/all_to_all | solution.py:582
  10.0 8.1 %collective-permute-start = (bf16[1,4,32,864]{3,2,1,0:T(8,128)(2,1)S(1)}, bf16[1,4,32,864]{3,2,1,0:T(8,128)(2,1)S(1)}, u32[]{:S(2)}, u32[]{:S(2)}) collective-permute-start(bf16[1,4,32,864]{3,2,1,0:T(8,128)(2,1)S(1)} %bitcast.6), channel_id=1, source_target_pairs={{0,16},{16,0},{1,17},{17,1},{2,18},{18,2},{3,19},{19,3},{4,20},{20... | collective-permute-start | bytes 663560 | tf_op jit(solution)/shard_map/ppermute | solution.py:560
  11.6 7.9 %collective-permute-start.1 = (bf16[1,32,128]{2,1,0:T(8,128)(2,1)S(1)}, bf16[1,32,128]{2,1,0:T(8,128)(2,1)S(1)}, u32[]{:S(2)}, u32[]{:S(2)}) collective-permute-start(bf16[1,32,128]{2,1,0:T(8,128)(2,1)S(1)} %get-tuple-element.23), channel_id=1, source_target_pairs={{0,16},{16,0},{1,17},{17,1},{2,18},{18,2},{3,19},{19,3},{4,20},{20... | collective-permute-start | bytes 24584 | tf_op jit(solution)/shard_map/ppermute | solution.py:560
  24.5 10.3 %copy-start = (bf16[1,4,3,384,128]{4,3,2,1,0:T(8,128)(2,1)S(1)}, bf16[1,4,3,384,128]{4,3,2,1,0:T(8,128)(2,1)}, u32[]{:S(2)}) copy-start(bf16[1,4,3,384,128]{4,3,2,1,0:T(8,128)(2,1)} %get-tuple-element.13.back_band) | copy-start | bytes 3538948

commit v3 on v2

--- a/solution.py
+++ b/solution.py
@@ -15,6 +15,7 @@
 FORWARD_MIB = 32
 BACKWARD_MIB = 24
 CHUNKS = 3
+BACK_CHUNKS = 2
 
 
 def round_up(value, step):
@@ -77,12 +78,12 @@
         xs[t, at, :] = jnp.where(first_half(), xs[t + 1, at, :], xs[t - 1, at, :])
 
 
-def convolve(xs, slots, matrix, plan, use):
+def convolve(xs, slots, matrix, plan, use, chunks=CHUNKS):
     rows = plan.rows
     mask = first_half()
-    step = plan.m // CHUNKS
+    step = plan.m // chunks
     row = lax.rem(lax.broadcasted_iota(jnp.int32, (step, 1), 0), rows)
-    for c in range(CHUNKS):
+    for c in range(chunks):
         parts = []
         for half, slot in enumerate(slots):
             if slot is None:
@@ -240,14 +241,15 @@
                 label_ref[at : at + rows, :] = jnp.where((lane < seen) | (lane == keep), piece, 0.0)
 
 
-def forward_steps(plan, buffers, matrix, base, keep):
+def forward_steps(plan, buffers, matrix, base, keep, filled=False):
     m, rows, group = plan.m, plan.rows, plan.group
     at = slice(rows, rows + m)
     count = plan.window
     source = buffers[0]
     for layer in range(plan.layers):
         target = buffers[1 + layer % 2]
-        fill_odd(source, range(1, (count - 4) // 2 + 1, 2), plan)
+        if layer > 0 or not filled:
+            fill_odd(source, range(1, (count - 4) // 2 + 1, 2), plan)
         keep(layer, source)
         count -= 2
         for b in range(round_up(count, group) // group):
@@ -314,7 +316,7 @@
 
     own_steps = forward_steps(plan, buffers, lambda layer, half: band[0, layer, half], base, keep)
     if plan.n_peer == 2:
-        other_steps = forward_steps(plan, others, lambda layer, half: other_band[0, layer, half], base, drop)
+        other_steps = forward_steps(plan, others, lambda layer, half: other_band[0, layer, half], base, drop, True)
         for unused in zip(own_steps, other_steps):
             pass
         for unused in other_steps:
@@ -364,7 +366,7 @@
     hidden_ref[...] = last[2, at, :]
 
     def other(q, carry):
-        for unused in forward_steps(plan, others, lambda layer, half: other_band[q, layer, half], base, drop):
+        for unused in forward_steps(plan, others, lambda layer, half: other_band[q, layer, half], base, drop, True):
             pass
         for g, u, share in other_share(q, last_of(others, plan)):
             part[:, columns_of(g, u)] = part[:, columns_of(g, u)] - share
@@ -461,7 +463,7 @@
                 else:
                     result[chunk, :] = total
 
-            convolve(level, slots, lambda half: back_band[0, layer, half], plan, use)
+            convolve(level, slots, lambda half: back_band[0, layer, half], plan, use, BACK_CHUNKS)
         level = target
 
     for d in range(plan.n_depth):

time: 68.7 us -> 68.7 us (level)
  no operation moved by 1% of the time
where the time goes in v3:
time: 68.7 us; the launch traced here: 68.4 us
  blocking collectives  27.5 us (40%)
  Pallas kernels  23 us (33%)
  starting transfers between devices  9.55 us (14%)
  waiting for transfers between devices  7.52 us (11%)
  between operations  0.72 us (1%)
    all_to_all x1, blocking collectives, body(): parts = lax.all_to_all(parts, GROUP, 0, 0, tiled=True)  15 us
    all_to_all x1, blocking collectives, body(): sums = lax.all_to_all(sums, GROUP, 0, 0, tiled=True)  12.5 us
    pallas_call x1, Pallas kernels, body(): call(forward_kernel, plan, [shape((layers, m, PAIR), BF16), shape((layers...  10.3 us
    all_to_all x1, starting transfers between devices, body(): slabs = lax.all_to_all(packed, GROUP, 0, 0, tiled=True)  7.4 us
    all_to_all x1, waiting for transfers between devices, body(): slabs = lax.all_to_all(packed, GROUP, 0, 0, tiled=True)  4.95 us
    pallas_call x2, Pallas kernels, make_bands(): call(lambda plan, *refs: band_kernel(plan, peers, backward, *refs), plan,...  4.75 us
    pallas_call x1, Pallas kernels, body(): call(backward_kernel, plan, shape((n, plan.back_rows, LANES), BF16), [plt...  4.58 us
    ppermute x2, waiting for transfers between devices, from_others(): lax.ppermute(array, 'peer', [(i, (i + q) % peers) for i in range(peers)])  2.57 us
  transfers between devices with their start and end apart: 3, of which 2 were waited for; matrix products, arithmetic and copies ran while one was open for 0% of the time, Pallas kernels for 7%

profile of v3, /device:TPU:0, one launch (start us, length us, event | category | flops | bytes accessed | tf_op | source)
XLA Modules:
  0.0 68.4 jit_solution(17826113270730939149)
XLA Ops:
  0.6 0.0 copy-start.1
  0.6 0.0 copy-start.2
  0.7 1.9 %shard_map.77 = bf16[16,128,128]{2,1,0:T(8,128)(2,1)} custom-call(s32[2,3]{1,0:T(2,128)} %bitcast.8, bf16[3,8,2048]{2,1,0:T(8,128)(2,1)} %feat_hbm.1, s32[3,8,64]{2,1,0:T(8,128)} %label_hbm.1), custom_call_target="tpu_custom_call" | custom-call | tf_op jit(solution)/shard_map/pallas_call | solution.py:572
  2.6 7.4 %all-to-all-start = ((bf16[16,128,128]{2,1,0:T(8,128)(2,1)}), bf16[16,128,128]{2,1,0:T(8,128)(2,1)S(1)}, u32[]{:S(2)}, u32[]{:S(2)}) async-start(bf16[16,128,128]{2,1,0:T(8,128)(2,1)} %shard_map.77), calls=%async_computation | async-start | bytes 1048576 | tf_op jit(solution)/shard_map/all_to_all | solution.py:584
  10.0 0.0 copy-done.1
  10.0 1.6 %collective-permute-start = (bf16[1,4,32,864]{3,2,1,0:T(8,128)(2,1)S(1)}, bf16[1,4,32,864]{3,2,1,0:T(8,128)(2,1)S(1)}, u32[]{:S(2)}, u32[]{:S(2)}) collective-permute-start(bf16[1,4,32,864]{3,2,1,0:T(8,128)(2,1)S(1)} %bitcast.6), channel_id=1, source_target_pairs={{0,16},{16,0},{1,17},{17,1},{2,18},{18,2},{3,19},{19,3},{4,20},{20... | collective-permute-start | bytes 663560 | tf_op jit(solution)/shard_map/ppermute | solution.py:562
  11.6 0.0 copy-done.2
  11.6 0.6 collective-permute-start.1
  12.2 3.4 %shard_map.76 = (bf16[1,4,3,384,128]{4,3,2,1,0:T(8,128)(2,1)S(1)}, bf16[1,4,3,384,128]{4,3,2,1,0:T(8,128)(2,1)}) custom-call(bf16[1,4,32,864]{3,2,1,0:T(8,128)(2,1)S(1)} %bitcast.7), custom_call_target="tpu_custom_call" | custom-call | flops 1000000000 | bytes 4000000 | tf_op jit(solution)/shard_map/pallas_call | solution.py:548
  15.5 2.6 %collective-permute-done.refs_0_ = bf16[1,4,32,864]{3,2,1,0:T(8,128)(2,1)S(1)} collective-permute-done((bf16[1,4,32,864]{3,2,1,0:T(8,128)(2,1)S(1)}, bf16[1,4,32,864]{3,2,1,0:T(8,128)(2,1)S(1)}, u32[]{:S(2)}, u32[]{:S(2)}) %collective-permute-start) | collective-permute-done | bytes 221216 | tf_op jit(solution)/shard_map/ppermute | solution.py:562
  18.1 1.4 %shard_map.78.other_band = bf16[1,4,3,384,128]{4,3,2,1,0:T(8,128)(2,1)S(1)} custom-call(bf16[1,4,32,864]{3,2,1,0:T(8,128)(2,1)S(1)} %collective-permute-done.refs_0_), custom_call_target="tpu_custom_call" | custom-call | flops 1000000000 | bytes 4000000 | tf_op jit(solution)/shard_map/pallas_call | solution.py:548
  19.5 0.0 collective-permute-done.1.heads_ref
  19.5 5.0 %all-to-all-done.recv_ref = bf16[16,128,128]{2,1,0:T(8,128)(2,1)S(1)} async-done(((bf16[16,128,128]{2,1,0:T(8,128)(2,1)}), bf16[16,128,128]{2,1,0:T(8,128)(2,1)S(1)}, u32[]{:S(2)}, u32[]{:S(2)}) %all-to-all-start) | async-done | bytes 524320 | tf_op jit(solution)/shard_map/all_to_all | solution.py:584
  24.5 0.0 copy-start
  24.5 10.3 %shard_map.79 = (bf16[4,384,256]{2,1,0:T(8,128)(2,1)S(1)}, bf16[4,3,384,128]{3,2,1,0:T(8,128)(2,1)S(1)}, bf16[384,1536]{1,0:T(8,128)(2,1)S(1)}, bf16[384,128]{1,0:T(8,128)(2,1)S(1)}) custom-call(bf16[16,128,128]{2,1,0:T(8,128)(2,1)S(1)} %all-to-all-done.recv_ref, bf16[1,4,3,384,128]{4,3,2,1,0:T(8,128)(2,1)S(1)} %get-tuple-element.14.band, ...), custom_call_target="tpu_custom_call" | custom-call | flops 8000000000 | bytes 10000000 | tf_op jit(solution)/shard_map/pallas_call | solution.py:593
  34.8 0.0 copy-done
  34.8 4.6 %shard_map.80 = bf16[16,80,128]{2,1,0:T(8,128)(2,1)S(1)} custom-call(bf16[1,4,3,384,128]{4,3,2,1,0:T(8,128)(2,1)S(1)} %copy-done, bf16[32,128]{1,0:T(8,128)(2,1)S(1)} %get-tuple-element.24.head_ref, bf16[4,384,256]{2,1,0:T(8,128)(2,1)S(1)} %get-tuple-element.15.acts, bf16[4,3,384,128]{3,2,1,0:T(8,128)(2,1)S(1)} %get-tuple-element.16.pres, ...), custom_call_target="tpu_custom_call" | custom-call | tf_op jit(solution)/shard_map/pallas_call | solution.py:611
  39.4 15.0 %all_to_all.15.recv_ref = bf16[16,80,128]{2,1,0:T(8,128)(2,1)S(1)} all-to-all(bf16[16,80,128]{2,1,0:T(8,128)(2,1)S(1)} %shard_map.80), channel_id=1, replica_groups=mesh['peer'=2,'depth'=4,'row'=4] {'depth','row'}, dimensions={0} | all-to-all | bytes 655360 | tf_op jit(solution)/shard_map/all_to_all | solution.py:625
  54.4 0.7 shard_map.81
  55.0 12.5 %all_to_all.16.recv_ref = bf16[16,56,128]{2,1,0:T(8,128)(2,1)S(1)} all-to-all(bf16[16,56,128]{2,1,0:T(8,128)(2,1)S(1)} %get-tuple-element.19), channel_id=1, replica_groups=mesh['peer'=2,'depth'=4,'row'=4] {'depth','row'}, dimensions={0} | all-to-all | bytes 458752 | tf_op jit(solution)/shard_map/all_to_all | solution.py:631
  67.6 0.8 %shard_map.82 = (f32[1,4,32,864]{3,2,1,0:T(8,128)}, f32[1,32,104]{2,1,0:T(8,128)}) custom-call(bf16[16,56,128]{2,1,0:T(8,128)(2,1)S(1)} %all_to_all.16.recv_ref), custom_call_target="tpu_custom_call" | custom-call | tf_op jit(solution)/shard_map/pallas_call | solution.py:632
  (1 shorter events, 0.0 us)
Async XLA Ops:
  0.6 9.4 %copy-start.1 = (bf16[1,4,864,32]{2,3,1,0:T(8,128)(2,1)S(1)}, bf16[1,4,864,32]{2,3,1,0:T(8,128)(2,1)}, u32[]{:S(2)}) copy-start(bf16[1,4,864,32]{2,3,1,0:T(8,128)(2,1)} %param.7) | copy-start | bytes 663556
  0.6 10.9 %copy-start.2 = (bf16[1,32,104]{2,1,0:T(8,128)(2,1)S(1)}, bf16[1,32,104]{2,1,0:T(8,128)(2,1)}, u32[]{:S(2)}) copy-start(bf16[1,32,104]{2,1,0:T(8,128)(2,1)} %param.8) | copy-start | bytes 19972
  2.6 21.9 %all-to-all-start = ((bf16[16,128,128]{2,1,0:T(8,128)(2,1)}), bf16[16,128,128]{2,1,0:T(8,128)(2,1)S(1)}, u32[]{:S(2)}, u32[]{:S(2)}) async-start(bf16[16,128,128]{2,1,0:T(8,128)(2,1)} %shard_map.77), calls=%async_computation | async-start | bytes 1048576 | tf_op jit(solution)/shard_map/all_to_all | solution.py:584
  10.0 8.1 %collective-permute-start = (bf16[1,4,32,864]{3,2,1,0:T(8,128)(2,1)S(1)}, bf16[1,4,32,864]{3,2,1,0:T(8,128)(2,1)S(1)}, u32[]{:S(2)}, u32[]{:S(2)}) collective-permute-start(bf16[1,4,32,864]{3,2,1,0:T(8,128)(2,1)S(1)} %bitcast.6), channel_id=1, source_target_pairs={{0,16},{16,0},{1,17},{17,1},{2,18},{18,2},{3,19},{19,3},{4,20},{20... | collective-permute-start | bytes 663560 | tf_op jit(solution)/shard_map/ppermute | solution.py:562
  11.6 7.9 %collective-permute-start.1 = (bf16[1,32,128]{2,1,0:T(8,128)(2,1)S(1)}, bf16[1,32,128]{2,1,0:T(8,128)(2,1)S(1)}, u32[]{:S(2)}, u32[]{:S(2)}) collective-permute-start(bf16[1,32,128]{2,1,0:T(8,128)(2,1)S(1)} %get-tuple-element.23), channel_id=1, source_target_pairs={{0,16},{16,0},{1,17},{17,1},{2,18},{18,2},{3,19},{19,3},{4,20},{20... | collective-permute-start | bytes 24584 | tf_op jit(solution)/shard_map/ppermute | solution.py:562
  24.5 10.3 %copy-start = (bf16[1,4,3,384,128]{4,3,2,1,0:T(8,128)(2,1)S(1)}, bf16[1,4,3,384,128]{4,3,2,1,0:T(8,128)(2,1)}, u32[]{:S(2)}) copy-start(bf16[1,4,3,384,128]{4,3,2,1,0:T(8,128)(2,1)} %get-tuple-element.13.back_band) | copy-start | bytes 3538948
